TPU v7x, 32 devices: a whole 2x2x4 slice. The times are simulated.
32 devices in a mesh: req: 8 (over z, x), ctx: 4 (over y, core).
Axes of the slice: x: 2, y: 2, z: 4, core: 2. Of those that a mesh axis runs over, the one named last changes fastest.
Arguments:
- item_table: bfloat16 [16384, 256], P('req'), may hold values from -6 to 6
- cand_owner: int32 [8, 512, 1], P('req'), may hold values from 0 to 7; in each aligned block of 128 rows (0 to 127, 128 to 255, ..., all dimensions but the last counted through in order) at most 32 rows name the same one
- cand_slot: int32 [8, 512], P('req'), may hold values from 0 to 2047
- w_in: bfloat16 [256, 1024], replicated, may hold values from -0.375 to 0.375
- w_uq: bfloat16 [1024, 2048], replicated, may hold values from -0.1875 to 0.1875
- w_out: bfloat16 [1024, 1024], replicated, may hold values from -0.1875 to 0.1875
- k_cache: bfloat16 [8, 16384, 1024], P('req', 'ctx'), may hold values from -12 to 12
- v_cache: bfloat16 [8, 16384, 1024], P('req', 'ctx'), may hold values from -6 to 6
- hist_len: int32 [8], P('req'), may hold values from 1024 to 16384, as said below
Outputs:
- ranked: bfloat16 [8, 512, 1024], P('req', 'ctx')
Inputs may be any that keep to these rules, and one draw needn't show every extreme that they name: `cand_owner`: in each aligned block of 512 / 4 candidates of a user, no owner is named more than 32 times, and in some block one owner is named exactly 32 times. `hist_len`: in every draw some user has the full 16384 events.
All inputs are finite; a program needn't handle non-finite values.
Results may differ from a plain program's by a relative error of at most 0.014.
Values may be sent and summed in bfloat16 or wider, within the bound.
No kernel may reach another device: no remote copies, remote signals or barrier semaphores. Data moves between devices by JAX's collectives and lax.ppermute only.
A program may use at most 128 MiB of HBM per device.

v0:
```python
import jax
import jax.numpy as jnp
from jax import lax
from jax.sharding import PartitionSpec as P

HEADS = 8


def layer_norm(values):
    centre = jnp.mean(values, axis=-1, keepdims=True)
    centred = values - centre
    spread = jnp.mean(centred * centred, axis=-1, keepdims=True)
    return centred * lax.rsqrt(spread + 1e-05)


def fetch_rows(owners, slot_ids, item_table, capacity):
    owner_count = lax.axis_size("req")
    matches = (owners[:, None] == jnp.arange(owner_count, dtype=jnp.int32)[None, :]).astype(
        jnp.int32
    )
    ranking = jnp.sum((jnp.cumsum(matches, axis=0) - 1) * matches, axis=1)
    outgoing = jnp.zeros((owner_count, capacity), jnp.int32).at[owners, ranking].set(slot_ids)
    looked_up = item_table[lax.all_to_all(outgoing, "req", split_axis=0, concat_axis=0, tiled=True)]
    returned = lax.all_to_all(looked_up, "req", split_axis=0, concat_axis=0, tiled=True)
    return returned[owners, ranking]


def attend_rows(queries, keys_local, values_local, length, offset):
    row_count, width = queries.shape
    head_dim = width // HEADS
    scale = head_dim ** (-0.5)
    block_keys = min(512, keys_local.shape[0])
    total_blocks = keys_local.shape[0] // block_keys
    query_heads = queries.reshape(row_count, HEADS, head_dim)

    def step(index, running):
        start = index * block_keys
        key_block = lax.dynamic_slice_in_dim(keys_local, start, block_keys, 0).reshape(
            block_keys, HEADS, head_dim
        )
        value_block = lax.dynamic_slice_in_dim(values_local, start, block_keys, 0).reshape(
            block_keys, HEADS, head_dim
        )
        scores = (
            jnp.einsum("qhd,khd->hqk", query_heads, key_block, preferred_element_type=jnp.float32)
            * scale
        )
        position = offset + start + jnp.arange(block_keys, dtype=jnp.int32)
        weights = jnp.where(position[None, None, :] < length, jax.nn.silu(scores), 0.0).astype(
            jnp.bfloat16
        )
        added = jnp.einsum("hqk,khd->qhd", weights, value_block, preferred_element_type=jnp.float32)
        return running + added.reshape(row_count, width)

    return lax.fori_loop(0, total_blocks, step, jnp.zeros((row_count, width), jnp.float32))


def shards(item_table, cand_owner, cand_slot, w_in, w_uq, w_out, k_cache, v_cache, hist_len):
    width = w_out.shape[0]
    ctx_count = lax.axis_size("ctx")
    ctx_index = lax.axis_index("ctx")
    per_device = cand_owner.shape[1] // ctx_count
    capacity_base = max(2, 2 * per_device // lax.axis_size("req"))
    owners_all = cand_owner[0, :, 0]
    slots_all = cand_slot[0]
    my_start = ctx_index * per_device
    my_owners = lax.dynamic_slice_in_dim(owners_all, my_start, per_device, 0)
    my_slots = lax.dynamic_slice_in_dim(slots_all, my_start, per_device, 0)
    embedded = fetch_rows(my_owners, my_slots, item_table, capacity_base)
    features = jnp.dot(embedded, w_in, preferred_element_type=jnp.float32).astype(jnp.bfloat16)
    normed = layer_norm(features.astype(jnp.float32)).astype(jnp.bfloat16)
    projected = jax.nn.silu(jnp.dot(normed, w_uq, preferred_element_type=jnp.float32)).astype(
        jnp.bfloat16
    )
    features, gate_u, query_mine = (features, projected[:, :width], projected[:, width:])
    queries = lax.all_gather(query_mine, "ctx", axis=0, tiled=True)
    length = hist_len[0]
    keys_local = k_cache[0]
    values_local = v_cache[0]
    offset = ctx_index * keys_local.shape[0]
    summed = lax.psum(attend_rows(queries, keys_local, values_local, length, offset), "ctx")
    attended = lax.dynamic_slice_in_dim(summed, my_start, per_device, 0)
    mixed = (layer_norm(attended) * gate_u.astype(jnp.float32)).astype(jnp.bfloat16)
    ranked = features.astype(jnp.float32) + jnp.dot(
        mixed, w_out, preferred_element_type=jnp.float32
    )
    return ranked.astype(jnp.bfloat16)[None]


def solution(mesh):
    in_specs = (
        P("req", None),
        P("req", None, None),
        P("req", None),
        P(),
        P(),
        P(),
        P("req", "ctx", None),
        P("req", "ctx", None),
        P("req"),
    )
    out_specs = P("req", "ctx", None)
    return jax.shard_map(shards, mesh=mesh, in_specs=in_specs, out_specs=out_specs, check_vma=False)
```

profile of v0, /device:TPU:0, one launch (start us, length us, event | category | flops | bytes accessed | tf_op | source)
XLA Modules:
  0.0 246.2 jit_solution(8199384177993119854)
XLA Ops:
  9.1 6.4 %scatter_fusion = s32[8,32]{1,0:T(8,128)S(1)} fusion(s32[8,32]{1,0:T(8,128)S(1)} %broadcast.132, s32[128]{0:T(128)S(1)} %get-tuple-element.189, s32[128]{0:T(128)S(1)} %fusion.24), kind=kCustom, calls=%fused_computation.2 | custom fusion | bytes 2560 | tf_op jit(solution)/shard_map/scatter | solution.py:22
  15.5 13.5 %all_to_all.17 = s32[8,1,32]{2,1,0:T(1,128)S(1)} all-to-all(s32[8,1,32]{2,1,0:T(1,128)S(1)} %bitcast.81), channel_id=1, replica_groups=mesh['req'=8,'ctx'=4] {'req'}, dimensions={0} | all-to-all | bytes 2048 | tf_op jit(solution)/shard_map/all_to_all | solution.py:23
  31.4 9.7 %all_to_all.18 = bf16[8,32,256]{2,1,0:T(8,128)(2,1)S(1)} all-to-all(bf16[8,32,256]{2,1,0:T(8,128)(2,1)S(1)} %bitcast.87), channel_id=1, replica_groups=mesh['req'=8,'ctx'=4] {'req'}, dimensions={0} | all-to-all | bytes 262144 | tf_op jit(solution)/shard_map/all_to_all | solution.py:24
  43.9 3.0 %multiply_convert_fusion = bf16[128,2048]{1,0:T(8,128)(2,1)S(1)} fusion(bf16[1024,2048]{1,0:T(8,128)(2,1)} %param.15, f32[128,1024]{1,0:T(8,128)S(1)} %get-tuple-element.194, f32[128]{0:T(128)S(1)} %add_rsqrt_fusion.1, f32[128]{0:T(128)S(1)} %broadcast_multiply_fusion.1), kind=kOutput, calls=%fused_computation.25 | convolution fusion | flops 538574848 | bytes 5243904 | tf_op jit(solution)/shard_map/dot_general | solution.py:72
  48.5 11.4 %copy.23 = bf16[1,4096,1024]{1,2,0:T(8,128)(2,1)} copy(bf16[1,4096,1024]{2,1,0:T(8,128)(2,1)} %param.18) | data formatting | bytes 16777216 | tf_op args[7]
  59.9 11.5 %copy.24 = bf16[1,4096,1024]{1,2,0:T(8,128)(2,1)} copy(bf16[1,4096,1024]{2,1,0:T(8,128)(2,1)} %param.17) | data formatting | bytes 16777216 | tf_op args[6]
  73.8 108.7 %while.14 = (s32[]{:T(128)}, f32[512,1024]{0,1:T(8,128)}, bf16[4096,1024]{0,1:T(8,128)(2,1)}, s32[]{:T(128)}, s32[]{:T(128)}, /*index=5*/bf16[4096,1024]{0,1:T(8...) while((s32[]{:T(128)}, f32[512,1024]{0,1:T(8,128)}, ...), condition=%wide.region_6.7_spmd.clone, body=%wide.region_5.6_spmd.clone.sunk | while | flops 1089471488 | bytes 15729853 | solution.py:55
  77.1 6.2 %fusion.46 = f32[8,128,512]{2,1,0:T(8,128)} fusion(bf16[512,8,128]{0,2,1:T(8,128)(2,1)} %bitcast.83, pred[512]{0:T(512)(128)(4,1)S(1)} %add_compare_fusion.2, bf16[512,8,128]{0,2,1:T(8,128)(2,1)S(1)} %bitcast.82, bf16[512,8,128]{2,0,1:T(8,128)(2,1)} %get-tuple-element.270), kind=kOutput, calls=%fused_computation.10.clone.1 | convolution fusion | flops 1088421888 | bytes 5243392 | tf_op jit(solution)/shard_map/while/body/eval_jaxpr/hqk,khd->qhd/dot_general | solution.py:52
  83.4 3.4 %bitcast_add_fusion.2 = f32[512,1024]{0,1:T(8,128)} fusion(f32[8,128,512]{2,1,0:T(8,128)} %fusion.46, f32[512,1024]{0,1:T(8,128)} %get-tuple-element.254, pred[]{:T(512)S(6)} %compare.13), kind=kLoop, calls=%fused_computation.12.clone.1 | loop fusion | flops 1048576 | bytes 6291457 | tf_op jit(solution)/shard_map/while/body/eval_jaxpr/add | solution.py:53
  90.2 6.3 %fusion.46 = f32[8,128,512]{2,1,0:T(8,128)} fusion(bf16[512,8,128]{0,2,1:T(8,128)(2,1)} %bitcast.83, pred[512]{0:T(512)(128)(4,1)S(1)} %add_compare_fusion.2, bf16[512,8,128]{0,2,1:T(8,128)(2,1)S(1)} %bitcast.82, bf16[512,8,128]{2,0,1:T(8,128)(2,1)} %get-tuple-element.270), kind=kOutput, calls=%fused_computation.10.clone.1 | convolution fusion | flops 1088421888 | bytes 5243392 | tf_op jit(solution)/shard_map/while/body/eval_jaxpr/hqk,khd->qhd/dot_general | solution.py:52
  96.4 4.1 %bitcast_add_fusion.2 = f32[512,1024]{0,1:T(8,128)} fusion(f32[8,128,512]{2,1,0:T(8,128)} %fusion.46, f32[512,1024]{0,1:T(8,128)} %get-tuple-element.254, pred[]{:T(512)S(6)} %compare.13), kind=kLoop, calls=%fused_computation.12.clone.1 | loop fusion | flops 1048576 | bytes 6291457 | tf_op jit(solution)/shard_map/while/body/eval_jaxpr/add | solution.py:53
  103.8 6.2 %fusion.46 = f32[8,128,512]{2,1,0:T(8,128)} fusion(bf16[512,8,128]{0,2,1:T(8,128)(2,1)} %bitcast.83, pred[512]{0:T(512)(128)(4,1)S(1)} %add_compare_fusion.2, bf16[512,8,128]{0,2,1:T(8,128)(2,1)S(1)} %bitcast.82, bf16[512,8,128]{2,0,1:T(8,128)(2,1)} %get-tuple-element.270), kind=kOutput, calls=%fused_computation.10.clone.1 | convolution fusion | flops 1088421888 | bytes 5243392 | tf_op jit(solution)/shard_map/while/body/eval_jaxpr/hqk,khd->qhd/dot_general | solution.py:52
  110.1 4.1 %bitcast_add_fusion.2 = f32[512,1024]{0,1:T(8,128)} fusion(f32[8,128,512]{2,1,0:T(8,128)} %fusion.46, f32[512,1024]{0,1:T(8,128)} %get-tuple-element.254, pred[]{:T(512)S(6)} %compare.13), kind=kLoop, calls=%fused_computation.12.clone.1 | loop fusion | flops 1048576 | bytes 6291457 | tf_op jit(solution)/shard_map/while/body/eval_jaxpr/add | solution.py:53
  117.5 6.2 %fusion.46 = f32[8,128,512]{2,1,0:T(8,128)} fusion(bf16[512,8,128]{0,2,1:T(8,128)(2,1)} %bitcast.83, pred[512]{0:T(512)(128)(4,1)S(1)} %add_compare_fusion.2, bf16[512,8,128]{0,2,1:T(8,128)(2,1)S(1)} %bitcast.82, bf16[512,8,128]{2,0,1:T(8,128)(2,1)} %get-tuple-element.270), kind=kOutput, calls=%fused_computation.10.clone.1 | convolution fusion | flops 1088421888 | bytes 5243392 | tf_op jit(solution)/shard_map/while/body/eval_jaxpr/hqk,khd->qhd/dot_general | solution.py:52
  123.8 4.1 %bitcast_add_fusion.2 = f32[512,1024]{0,1:T(8,128)} fusion(f32[8,128,512]{2,1,0:T(8,128)} %fusion.46, f32[512,1024]{0,1:T(8,128)} %get-tuple-element.254, pred[]{:T(512)S(6)} %compare.13), kind=kLoop, calls=%fused_computation.12.clone.1 | loop fusion | flops 1048576 | bytes 6291457 | tf_op jit(solution)/shard_map/while/body/eval_jaxpr/add | solution.py:53
  131.2 6.2 %fusion.46 = f32[8,128,512]{2,1,0:T(8,128)} fusion(bf16[512,8,128]{0,2,1:T(8,128)(2,1)} %bitcast.83, pred[512]{0:T(512)(128)(4,1)S(1)} %add_compare_fusion.2, bf16[512,8,128]{0,2,1:T(8,128)(2,1)S(1)} %bitcast.82, bf16[512,8,128]{2,0,1:T(8,128)(2,1)} %get-tuple-element.270), kind=kOutput, calls=%fused_computation.10.clone.1 | convolution fusion | flops 1088421888 | bytes 5243392 | tf_op jit(solution)/shard_map/while/body/eval_jaxpr/hqk,khd->qhd/dot_general | solution.py:52
  137.4 4.1 %bitcast_add_fusion.2 = f32[512,1024]{0,1:T(8,128)} fusion(f32[8,128,512]{2,1,0:T(8,128)} %fusion.46, f32[512,1024]{0,1:T(8,128)} %get-tuple-element.254, pred[]{:T(512)S(6)} %compare.13), kind=kLoop, calls=%fused_computation.12.clone.1 | loop fusion | flops 1048576 | bytes 6291457 | tf_op jit(solution)/shard_map/while/body/eval_jaxpr/add | solution.py:53
  144.8 6.2 %fusion.46 = f32[8,128,512]{2,1,0:T(8,128)} fusion(bf16[512,8,128]{0,2,1:T(8,128)(2,1)} %bitcast.83, pred[512]{0:T(512)(128)(4,1)S(1)} %add_compare_fusion.2, bf16[512,8,128]{0,2,1:T(8,128)(2,1)S(1)} %bitcast.82, bf16[512,8,128]{2,0,1:T(8,128)(2,1)} %get-tuple-element.270), kind=kOutput, calls=%fused_computation.10.clone.1 | convolution fusion | flops 1088421888 | bytes 5243392 | tf_op jit(solution)/shard_map/while/body/eval_jaxpr/hqk,khd->qhd/dot_general | solution.py:52
  151.1 4.1 %bitcast_add_fusion.2 = f32[512,1024]{0,1:T(8,128)} fusion(f32[8,128,512]{2,1,0:T(8,128)} %fusion.46, f32[512,1024]{0,1:T(8,128)} %get-tuple-element.254, pred[]{:T(512)S(6)} %compare.13), kind=kLoop, calls=%fused_computation.12.clone.1 | loop fusion | flops 1048576 | bytes 6291457 | tf_op jit(solution)/shard_map/while/body/eval_jaxpr/add | solution.py:53
  158.5 6.2 %fusion.46 = f32[8,128,512]{2,1,0:T(8,128)} fusion(bf16[512,8,128]{0,2,1:T(8,128)(2,1)} %bitcast.83, pred[512]{0:T(512)(128)(4,1)S(1)} %add_compare_fusion.2, bf16[512,8,128]{0,2,1:T(8,128)(2,1)S(1)} %bitcast.82, bf16[512,8,128]{2,0,1:T(8,128)(2,1)} %get-tuple-element.270), kind=kOutput, calls=%fused_computation.10.clone.1 | convolution fusion | flops 1088421888 | bytes 5243392 | tf_op jit(solution)/shard_map/while/body/eval_jaxpr/hqk,khd->qhd/dot_general | solution.py:52
  164.8 4.1 %bitcast_add_fusion.2 = f32[512,1024]{0,1:T(8,128)} fusion(f32[8,128,512]{2,1,0:T(8,128)} %fusion.46, f32[512,1024]{0,1:T(8,128)} %get-tuple-element.254, pred[]{:T(512)S(6)} %compare.13), kind=kLoop, calls=%fused_computation.12.clone.1 | loop fusion | flops 1048576 | bytes 6291457 | tf_op jit(solution)/shard_map/while/body/eval_jaxpr/add | solution.py:53
  172.2 6.2 %fusion.46 = f32[8,128,512]{2,1,0:T(8,128)} fusion(bf16[512,8,128]{0,2,1:T(8,128)(2,1)} %bitcast.83, pred[512]{0:T(512)(128)(4,1)S(1)} %add_compare_fusion.2, bf16[512,8,128]{0,2,1:T(8,128)(2,1)S(1)} %bitcast.82, bf16[512,8,128]{2,0,1:T(8,128)(2,1)} %get-tuple-element.270), kind=kOutput, calls=%fused_computation.10.clone.1 | convolution fusion | flops 1088421888 | bytes 5243392 | tf_op jit(solution)/shard_map/while/body/eval_jaxpr/hqk,khd->qhd/dot_general | solution.py:52
  178.4 4.1 %bitcast_add_fusion.2 = f32[512,1024]{0,1:T(8,128)} fusion(f32[8,128,512]{2,1,0:T(8,128)} %fusion.46, f32[512,1024]{0,1:T(8,128)} %get-tuple-element.254, pred[]{:T(512)S(6)} %compare.13), kind=kLoop, calls=%fused_computation.12.clone.1 | loop fusion | flops 1048576 | bytes 6291457 | tf_op jit(solution)/shard_map/while/body/eval_jaxpr/add | solution.py:53
  185.5 49.2 %all-reduce.2.cloned.1.call-done = f32[512,1024]{1,0:T(8,128)} async-done(((f32[512,1024]{1,0:T(8,128)}), f32[512,1024]{1,0:T(8,128)}) %all-reduce.2.cloned.1.call-update) | async-done | bytes 2097168 | tf_op jit(solution)/shard_map/psum | solution.py:81
  (56 shorter events, 46.1 us)
Async XLA Ops:
  6.5 230.6 %copy-start = (bf16[1024,1024]{1,0:T(8,128)(2,1)S(1)}, bf16[1024,1024]{1,0:T(8,128)(2,1)}, u32[]{:S(2)}) copy-start(bf16[1024,1024]{1,0:T(8,128)(2,1)} %param.16) | copy-start | bytes 6291460
  6.5 64.8 %all-gather.2.cloned.1.call-start = ((), (), s32[]{:S(2)}) async-start(), calls=%async_computation.2 | async-start | bytes 1310720 | tf_op jit(solution)/shard_map/all_gather | solution.py:76
  43.6 3.3 %copy-start.1 = (f32[128,1024]{1,0:T(8,128)}, f32[128,1024]{1,0:T(8,128)S(1)}, u32[]{:S(2)}) copy-start(f32[128,1024]{1,0:T(8,128)S(1)} %get-tuple-element.194) | copy-start | bytes 1572868
  46.9 0.8 copy-start.3
  48.5 186.2 %all-reduce.2.cloned.1.call-start = ((), (), s32[]{:S(2)}) async-start(), calls=%async_computation.3 | async-start | bytes 4194304 | tf_op jit(solution)/shard_map/psum | solution.py:81
  182.5 54.6 %copy-start.2 = (f32[128,1024]{1,0:T(8,128)S(1)}, f32[128,1024]{1,0:T(8,128)}, u32[]{:S(2)}) copy-start(f32[128,1024]{1,0:T(8,128)} %copy-done.1) | copy-start | bytes 1572868
  182.5 54.6 %copy-start.4 = (bf16[128,2048]{1,0:T(8,128)(2,1)S(1)}, bf16[128,2048]{1,0:T(8,128)(2,1)}, u32[]{:S(2)}) copy-start(bf16[128,2048]{1,0:T(8,128)(2,1)} %copy-done.3) | copy-start | bytes 1572868
Sparse Core Ops, SparseCore 0:
  48.6 14.5 all-gather.1
  185.6 49.0 all-reduce.1
where the time goes:
time: 248 us; the launch traced here: 246 us
  local copies, waits for them, and re-layouts  62.7 us (25%)
  matrix products  56.6 us (23%)
  waiting for transfers between devices  49.2 us (20%)
  other arithmetic  40.8 us (16%)
  blocking collectives  23.3 us (9%)
  between operations  13.5 us (5%)
    dot_general x8, matrix products, step(): jnp.einsum('hqk,khd->qhd', weights, value_block, preferred_element_type=j...  50 us
    psum x1, waiting for transfers between devices, shards(): lax.psum(attend_rows(queries, keys_local, values_local, length, offset),...  49.2 us
    add x8, other arithmetic, step(): return running + added.reshape(row_count, width)  31.9 us
    unnamed x13, local copies, waits for them, and re-layouts  26.1 us
    dynamic_slice x8, local copies, waits for them, and re-layouts, step(): lax.dynamic_slice_in_dim(keys_local, start, block_keys, 0)  21.6 us
    all_to_all x1, blocking collectives, fetch_rows(): lax.all_to_all(outgoing, 'req', split_axis=0, concat_axis=0, tiled=True)  13.5 us
    all_to_all x1, blocking collectives, fetch_rows(): lax.all_to_all(looked_up, 'req', split_axis=0, concat_axis=0, tiled=True)  9.74 us
    scatter x1, local copies, waits for them, and re-layouts, fetch_rows(): jnp.zeros((owner_count, capacity), jnp.int32).at[owners, ranking]  6.36 us
  transfers between devices with their start and end apart: 2, of which 1 were waited for; matrix products, arithmetic and copies ran while one was open for 9% of the time, Pallas kernels for 0%

commit v1 on v0

v1 whole, which is shorter than its diff:
```python
import functools

import jax
import jax.numpy as jnp
from jax import lax
from jax.experimental import pallas as pl
from jax.experimental.pallas import tpu as pltpu
from jax.sharding import PartitionSpec as P

HEADS = 8
KEY_BLOCK = 256
GROUP = 1024
VMEM = pl.BlockSpec(memory_space=pltpu.VMEM)
SMEM = pl.BlockSpec(memory_space=pltpu.SMEM)
F32 = jnp.float32
BF16 = jnp.bfloat16
NT = (((1,), (1,)), ((), ()))


def params(mib):
    return pltpu.CompilerParams(vmem_limit_bytes=mib << 20)


def layer_norm(values):
    centre = jnp.mean(values, axis=-1, keepdims=True)
    centred = values - centre
    spread = jnp.mean(centred * centred, axis=-1, keepdims=True)
    return centred * lax.rsqrt(spread + 1e-05)


def silu(values):
    half = values * 0.5
    return half + half * jnp.tanh(half)


def dot(a, b):
    return jnp.dot(a, b, preferred_element_type=F32)


def iota(shape, axis):
    return lax.broadcasted_iota(jnp.int32, shape, axis)


def hi_lo(row):
    wide = jnp.broadcast_to(row, (8, row.shape[1]))
    pick = iota(wide.shape, 0)
    parts = jnp.where(pick == 0, wide >> 8, jnp.where(pick == 1, wide & 255, 0))
    return parts.astype(F32).astype(BF16)


def ranks(owners, per):
    count = owners.shape[1]
    owner_count = lax.axis_size("req")
    codes = owners ^ lax.axis_index("req")
    named = iota((owner_count, count), 0) == codes
    row, column = iota((count, count), 0), iota((count, count), 1)
    earlier = ((row // per == column // per) & (row < column)).astype(F32).astype(BF16)
    before = dot(named.astype(F32).astype(BF16), earlier)
    rank = jnp.sum(jnp.where(named, before, 0.0), axis=0, keepdims=True)
    return codes, rank.astype(jnp.int32)


def code_of(peer, turn, peers):
    return turn * peers + (peer if turn % 2 == 0 else peers - 1 - peer)


def requests_kernel(per, cap, turns, owners_ref, slots_ref, *list_refs):
    peers = lax.axis_size("ctx")
    codes, rank = ranks(owners_ref[...], per)
    place = (iota(codes.shape, 1) // per) * cap + rank
    parts = hi_lo(slots_ref[...])
    length = peers * cap
    for turn in range(turns):
        code = code_of(lax.axis_index("ctx"), turn, peers)
        wanted = jnp.where(codes == code, place, -1)
        chosen = (iota((length, codes.shape[1]), 0) == wanted).astype(F32).astype(BF16)
        packed = lax.dot_general(parts, chosen, NT, preferred_element_type=F32)
        packed = packed[0:1] * 256.0 + packed[1:2]
        list_refs[turn][...] = packed.astype(jnp.int32)


def block_order(peers):
    return list(range(0, peers, 2)) + list(range(1, peers, 2))


def places_kernel(per, cap, turns, owners_ref, places_ref):
    peers = lax.axis_size("ctx")
    me = lax.axis_index("ctx")
    codes, rank = ranks(owners_ref[...], per)
    count = codes.shape[1]
    length = peers * cap
    turn = codes // peers
    inner = codes % peers
    peer = jnp.where(turn % 2 == 0, inner, peers - 1 - inner) ^ me
    buffer = jnp.zeros_like(peer)
    for bit, step in enumerate(exchange_steps(peers)):
        buffer = buffer + jnp.where((peer & step) != 0, 1 << bit, 0)
    place = (buffer * turns + turn) * length + (iota(codes.shape, 1) // per) * cap + rank
    row, column = iota((count, count), 0), iota((count, count), 1)
    block = row // per
    half = peers // 2
    relative = jnp.where(block < half, 2 * block, 2 * (block - half) + 1)
    source = (relative ^ me) * per + row % per
    order = (source == column).astype(F32).astype(BF16)
    found = lax.dot_general(order, hi_lo(place), NT, preferred_element_type=F32)
    found = (found[:, 0:1] * 256.0 + found[:, 1:2]).astype(jnp.int32)
    total = places_ref.shape[1]
    places_ref[...] = (iota((count, total), 1) == found).astype(F32).astype(BF16)


def exchange_steps(peers):
    steps, step = [], peers // 2
    while step >= 1:
        steps.append(step)
        step //= 2
    return steps


def lookup_kernel(list_ref, table_ref, rows_ref):
    length = list_ref.shape[1]
    same = (iota((length, length), 0) == iota((length, length), 1)).astype(F32).astype(BF16)
    found = lax.dot_general(same, hi_lo(list_ref[...]), NT, preferred_element_type=F32)
    found = (found[:, 0:1] * 256.0 + found[:, 1:2]).astype(jnp.int32)
    chosen = (iota((length, table_ref.shape[0]), 1) == found).astype(F32).astype(BF16)
    rows_ref[...] = dot(chosen, table_ref[...]).astype(BF16)


def project_kernel(per, buffers, *refs):
    places_ref, w_in_ref, w_uq_ref = refs[0], refs[1 + buffers], refs[2 + buffers]
    features_ref, gate_ref, query_ref = refs[3 + buffers :]
    width = w_in_ref.shape[1]
    embedded = None
    start = 0
    for received in refs[1 : 1 + buffers]:
        rows = received.shape[0]
        part = dot(places_ref[:, start : start + rows], received[...])
        embedded = part if embedded is None else embedded + part
        start += rows
    features = dot(embedded.astype(BF16), w_in_ref[...]).astype(BF16)
    features_ref[...] = features[:per]
    normed = layer_norm(features.astype(F32)).astype(BF16)
    query_ref[...] = silu(dot(normed, w_uq_ref[:, width:])).astype(BF16)
    gate_ref[...] = silu(dot(normed[:per], w_uq_ref[:, :width])).astype(BF16)


def attend_kernel(length_ref, query_ref, key_ref, value_ref, keep_ref, send_ref):
    events, head_dim = key_ref.shape
    scale = 0.5 * head_dim ** (-0.5)
    group = min(GROUP, events)
    block = min(KEY_BLOCK, group)
    valid = length_ref[0] - lax.axis_index("ctx") * events
    queries = query_ref[...]
    kept = keep_ref.shape[0]

    def add_group(first, total, masked):
        for inner in range(group // block):
            start = first + inner * block
            if not isinstance(start, int):
                start = pl.multiple_of(start, block)
            keys = key_ref[pl.ds(start, block), :]
            values = value_ref[pl.ds(start, block), :]
            if masked:
                inside = (iota((block, head_dim), 0) + start) < valid
                values = jnp.where(inside, values.astype(F32), 0.0).astype(BF16)
            half = lax.dot_general(queries, keys, NT, preferred_element_type=F32) * scale
            weights = (half + half * jnp.tanh(half)).astype(BF16)
            total = total + dot(weights, values)
        return total

    def store(total):
        keep_ref[...] = total[:kept]
        send_ref[...] = total[kept:].astype(BF16)

    zero = jnp.zeros((queries.shape[0], head_dim), F32)

    @pl.when(valid > events - group)
    def _():
        total = zero
        for first in range(0, events, group):
            total = add_group(first, total, first + group >= events)
        store(total)

    @pl.when(valid <= events - group)
    def _():
        trips = jnp.maximum(valid + group - 1, 0) // group
        store(lax.fori_loop(0, trips, lambda i, t: add_group(i * group, t, True), zero))


def finish_kernel(others, *refs):
    keep_ref, sibling_ref = refs[:2]
    gate_ref, features_ref, w_out_ref, out_ref = refs[2 + others :]
    attended = keep_ref[...] + sibling_ref[...].astype(F32)
    for other in refs[2 : 2 + others]:
        attended = attended + other[...].astype(F32)
    mixed = (layer_norm(attended) * gate_ref[...].astype(F32)).astype(BF16)
    ranked = features_ref[...].astype(F32) + dot(mixed, w_out_ref[...])
    out_ref[...] = ranked.astype(BF16)


def shards(item_table, cand_owner, cand_slot, w_in, w_uq, w_out, k_cache, v_cache, hist_len):
    users, peers = lax.axis_size("req"), lax.axis_size("ctx")
    count = cand_owner.shape[1]
    per = count // peers
    cap = max(2, 2 * per // users)
    turns = users // peers
    length = peers * cap
    width = w_out.shape[0]
    shape = jax.ShapeDtypeStruct

    def permute(values, target):
        pairs = []
        for user in range(users):
            for peer in range(peers):
                to_user, to_peer = target(user, peer)
                pairs.append((user * peers + peer, to_user * peers + to_peer))
        return lax.ppermute(values, ("req", "ctx"), pairs)

    def swap_owner(values, turn):
        return permute(values, lambda user, peer: (user ^ code_of(peer, turn, peers), peer))

    def swap_peer(values, step):
        return permute(values, lambda user, peer: (user, peer ^ step))

    owners = cand_owner.reshape(1, count)
    slots = cand_slot.reshape(1, count)
    lists = pl.pallas_call(
        functools.partial(requests_kernel, per, cap, turns),
        in_specs=[VMEM] * 2,
        out_specs=[VMEM] * turns,
        out_shape=[shape((1, length), jnp.int32)] * turns,
        compiler_params=params(16),
        name="requests",
    )(owners, slots)
    asked = [swap_owner(one, turn) for turn, one in enumerate(lists)]
    places = pl.pallas_call(
        functools.partial(places_kernel, per, cap, turns),
        in_specs=[VMEM],
        out_specs=VMEM,
        out_shape=shape((count, users * length), BF16),
        compiler_params=params(16),
        name="places",
    )(owners)
    rows = []
    for turn in range(turns):
        looked = pl.pallas_call(
            lookup_kernel,
            in_specs=[VMEM] * 2,
            out_specs=VMEM,
            out_shape=shape((length, item_table.shape[1]), BF16),
            compiler_params=params(16),
            name="lookup",
        )(asked[turn], item_table)
        rows.append(swap_owner(looked, turn))
    buffers = [jnp.concatenate(rows, axis=0)]
    for step in exchange_steps(peers):
        buffers = buffers + [swap_peer(one, step) for one in buffers]
    features, gate, queries = pl.pallas_call(
        functools.partial(project_kernel, per, len(buffers)),
        in_specs=[VMEM] * (3 + len(buffers)),
        out_specs=[VMEM] * 3,
        out_shape=[
            shape((per, width), BF16),
            shape((per, width), BF16),
            shape((count, width), BF16),
        ],
        compiler_params=params(32),
        name="project",
    )(places, *buffers, w_in, w_uq)
    keys, values = k_cache[0], v_cache[0]
    events = keys.shape[0]
    head_dim = width // HEADS
    half = count // 2
    keep, send = pl.pallas_call(
        attend_kernel,
        grid=(HEADS,),
        in_specs=[SMEM]
        + [pl.BlockSpec((rows_of, head_dim), lambda h: (0, h)) for rows_of in (count, events, events)],
        out_specs=[pl.BlockSpec((half, head_dim), lambda h: (0, h))] * 2,
        out_shape=[shape((half, width), F32), shape((half, width), BF16)],
        compiler_params=params(48),
        name="attend",
    )(hist_len, queries, keys, values)
    sibling = swap_peer(send, 1)
    others = []
    for index in range(1, peers // 2):
        piece = slice(index * per, (index + 1) * per)
        summed = (keep[piece] + sibling[piece].astype(F32)).astype(BF16)
        others.append(swap_peer(summed, 2 * index))
    ranked = pl.pallas_call(
        functools.partial(finish_kernel, len(others)),
        grid=(1,),
        in_specs=[pl.BlockSpec((per, width), lambda i: (0, 0))] * (4 + len(others))
        + [pl.BlockSpec((width, width), lambda i: (0, 0))],
        out_specs=pl.BlockSpec((per, width), lambda i: (0, 0)),
        out_shape=shape((per, width), BF16),
        compiler_params=params(24),
        name="finish",
    )(keep, sibling, *others, gate, features, w_out)
    return ranked[None]


def solution(mesh):
    in_specs = (
        P("req", None),
        P("req", None, None),
        P("req", None),
        P(),
        P(),
        P(),
        P("req", "ctx", None),
        P("req", "ctx", None),
        P("req"),
    )
    out_specs = P("req", "ctx", None)
    return jax.shard_map(shards, mesh=mesh, in_specs=in_specs, out_specs=out_specs, check_vma=False)
```

time: 248 us -> 76.6 us (0.31)
  matrix products: 56.6 us -> 0 us
  local copies, waits for them, and re-layouts: 62.7 us -> 7.73 us
  other arithmetic: 40.8 us -> 0.05 us
  waiting for transfers between devices: 49.2 us -> 17 us
  Pallas kernels: 0 us -> 29.6 us
  blocking collectives: 23.3 us -> 0 us
  starting transfers between devices: 0.04 us -> 20.4 us
  between operations: 13.5 us -> 0.79 us
    dot_general x11 -> x0, matrix products: 56.6 us -> none  [the longest x8 50 us: step(): jnp.einsum('hqk,khd->qhd', weights, value_block, preferred_element_type=j...]
    psum x1 -> x0, waiting for transfers between devices: 49.2 us -> none  [shards(): lax.psum(attend_rows(queries, keys_local, values_local, length, offset),...]
    add x8 -> x0, other arithmetic: 31.9 us -> none  [step(): return running + added.reshape(row_count, width)]
    pallas_call x0 -> x7, Pallas kernels: none -> 29.6 us  [the longest x1 22.8 us: shards(): pl.pallas_call(attend_kernel, grid=(HEADS,), in_specs=[SMEM] + [pl.BlockS...]
    all_to_all x2 -> x0, blocking collectives: 23.3 us -> none  [the longest x1 13.5 us: fetch_rows(): lax.all_to_all(outgoing, 'req', split_axis=0, concat_axis=0, tiled=True)]
    dynamic_slice x9 -> x0, local copies, waits for them, and re-layouts: 22.2 us -> none  [the longest x8 21.6 us: step(): lax.dynamic_slice_in_dim(keys_local, start, block_keys, 0)]
    ppermute x0 -> x9, starting transfers between devices: none -> 20.4 us  [permute(): return lax.ppermute(values, ('req', 'ctx'), pairs)]
    unnamed x13 -> x17, local copies, waits for them, and re-layouts: 26.1 us -> 7.72 us
  transfers between devices with their start and end apart: 2 -> 9, of which waited for: 1 -> 5; matrix products, arithmetic and copies ran while one was open for 9% -> 0% of each run, Pallas kernels for 0% -> 2%
where the time goes in v1:
time: 76.6 us; the launch traced here: 75.6 us
  Pallas kernels  29.6 us (39%)
  starting transfers between devices  20.4 us (27%)
  waiting for transfers between devices  17 us (22%)
  local copies, waits for them, and re-layouts  7.73 us (10%)
  between operations  0.79 us (1%)
    pallas_call x1, Pallas kernels, shards(): pl.pallas_call(attend_kernel, grid=(HEADS,), in_specs=[SMEM] + [pl.BlockS...  22.8 us
    ppermute x9, starting transfers between devices, permute(): return lax.ppermute(values, ('req', 'ctx'), pairs)  20.4 us
    ppermute x9, waiting for transfers between devices, permute(): return lax.ppermute(values, ('req', 'ctx'), pairs)  17 us
    unnamed x17, local copies, waits for them, and re-layouts  7.72 us
    pallas_call x1, Pallas kernels, shards(): pl.pallas_call(functools.partial(project_kernel, per, len(buffers)), in_s...  3.25 us
  transfers between devices with their start and end apart: 9, of which 5 were waited for; matrix products, arithmetic and copies ran while one was open for 0% of the time, Pallas kernels for 2%

profile of v1, /device:TPU:0, one launch (start us, length us, event | category | flops | bytes accessed | tf_op | source)
XLA Modules:
  0.0 75.6 jit_solution(16706422035897863798)
XLA Ops:
  0.0 0.7 copy-done.5
  0.7 0.7 copy-done.7
  1.4 0.4 requests.1
  1.7 0.7 collective-permute-start
  2.4 1.2 %copy-done.1 = bf16[2048,256]{1,0:T(8,128)(2,1)S(1)} copy-done((bf16[2048,256]{1,0:T(8,128)(2,1)S(1)}, bf16[2048,256]{1,0:T(8,128)(2,1)}, u32[]{:S(2)}) %copy-start.1) | copy-done | bytes 1048600
  3.6 0.6 lookup.2
  4.2 0.7 collective-permute-start.1
  4.9 6.0 %collective-permute-start.2 = (s32[1,128]{1,0:T(1,128)S(1)}, s32[1,128]{1,0:T(1,128)S(1)}, u32[]{:S(2)}, u32[]{:S(2)}) collective-permute-start(s32[1,128]{1,0:T(1,128)S(1)} %get-tuple-element.13), channel_id=1, source_target_pairs={{0,28},{1,25},{2,22},{3,19},{4,24},{5,29},{6,18},{7,23},{8,20},{9,... | collective-permute-start | bytes 1544 | tf_op jit(solution)/shard_map/ppermute | solution.py:216
  10.9 1.5 %collective-permute-done.2.list_ref = s32[1,128]{1,0:T(1,128)S(1)} collective-permute-done((s32[1,128]{1,0:T(1,128)S(1)}, s32[1,128]{1,0:T(1,128)S(1)}, u32[]{:S(2)}, u32[]{:S(2)}) %collective-permute-start.2) | collective-permute-done | bytes 544 | tf_op jit(solution)/shard_map/ppermute | solution.py:216
  12.5 1.2 %copy-done.2 = bf16[2048,256]{1,0:T(8,128)(2,1)S(1)} copy-done((bf16[2048,256]{1,0:T(8,128)(2,1)S(1)}, bf16[2048,256]{1,0:T(8,128)(2,1)}, u32[]{:S(2)}) %copy-start.2) | copy-done | bytes 1048600
  13.7 0.6 lookup.3
  14.3 4.8 %collective-permute-start.3 = (bf16[128,256]{1,0:T(8,128)(2,1)S(1)}, bf16[128,256]{1,0:T(8,128)(2,1)S(1)}, u32[]{:S(2)}, u32[]{:S(2)}) collective-permute-start(bf16[128,256]{1,0:T(8,128)(2,1)S(1)} %lookup.3), channel_id=1, source_target_pairs={{0,28},{1,25},{2,22},{3,19},{4,24},{5,29},{6,18},{7,23},{8,20},{9,... | collective-permute-start | bytes 196616 | tf_op jit(solution)/shard_map/ppermute | solution.py:216
  19.1 2.3 %collective-permute-done.3 = bf16[128,256]{1,0:T(8,128)(2,1)S(1)} collective-permute-done((bf16[128,256]{1,0:T(8,128)(2,1)S(1)}, bf16[128,256]{1,0:T(8,128)(2,1)S(1)}, u32[]{:S(2)}, u32[]{:S(2)}) %collective-permute-start.3) | collective-permute-done | bytes 65568 | tf_op jit(solution)/shard_map/ppermute | solution.py:216
  21.4 8.1 %collective-permute-start.4 = (bf16[256,256]{1,0:T(8,128)(2,1)S(1)}, bf16[256,256]{1,0:T(8,128)(2,1)S(1)}, u32[]{:S(2)}, u32[]{:S(2)}) collective-permute-start(bf16[256,256]{1,0:T(8,128)(2,1)S(1)} %constant_dynamic-update-slice_fusion.refs_1_), channel_id=1, source_target_pairs={{0,2},{1,3},{2,0},{3,1},{4,6},{5,7},{6,4},{7,5},{8,10},{9,11},{10,... | collective-permute-start | bytes 393224 | tf_op jit(solution)/shard_map/ppermute | solution.py:216
  29.5 2.9 %collective-permute-done.4.refs_2_ = bf16[256,256]{1,0:T(8,128)(2,1)S(1)} collective-permute-done((bf16[256,256]{1,0:T(8,128)(2,1)S(1)}, bf16[256,256]{1,0:T(8,128)(2,1)S(1)}, u32[]{:S(2)}, u32[]{:S(2)}) %collective-permute-start.4) | collective-permute-done | bytes 131104 | tf_op jit(solution)/shard_map/ppermute | solution.py:216
  32.4 0.7 copy-done.6
  33.1 0.7 places.1.refs_0_
  34.5 2.2 %copy-done = bf16[1024,2048]{1,0:T(8,128)(2,1)S(1)} copy-done((bf16[1024,2048]{1,0:T(8,128)(2,1)S(1)}, bf16[1024,2048]{1,0:T(8,128)(2,1)}, u32[]{:S(2)}) %copy-start) | copy-done | bytes 4194328
  36.7 1.0 %copy-done.4 = bf16[256,1024]{1,0:T(8,128)(2,1)S(1)} copy-done((bf16[256,1024]{1,0:T(8,128)(2,1)S(1)}, bf16[256,1024]{1,0:T(8,128)(2,1)}, u32[]{:S(2)}) %copy-start.4) | copy-done | bytes 524312
  37.7 3.3 %project.1 = (bf16[128,1024]{1,0:T(8,128)(2,1)S(1)}, bf16[128,1024]{1,0:T(8,128)(2,1)S(1)}, bf16[512,1024]{1,0:T(8,128)(2,1)S(1)}) custom-call(bf16[512,1024]{1,0:T(8,128)(2,1)S(1)} %places.1.refs_0_, bf16[256,256]{1,0:T(8,128)(2,1)S(1)} %constant_dynamic-update-slice_fusion.refs_1_, bf16[256,256]{1,0:T(8,128)(2,1)S(1)} %collective-permute-done.4.refs_2_, ...), custom_call_target="tpu_custom_call" | custom-call | tf_op jit(solution)/shard_map/project/pallas_call | solution.py:257
  41.0 22.8 %attend.1 = (f32[256,1024]{1,0:T(8,128)S(1)}, bf16[256,1024]{1,0:T(8,128)(2,1)S(1)}) custom-call(s32[1]{0:T(128)S(6)} %copy.11.length_ref, bf16[512,1024]{1,0:T(8,128)(2,1)S(1)} %get-tuple-element.14.query_ref, bf16[4096,1024]{1,0:T(8,128)(2,1)} %bitcast.6, bf16[4096,1024]{1,0:T(8,128)(2,1)} %bitcast.7), custom_call_target="tpu_custom_call" | custom-call | tf_op jit(solution)/shard_map/attend/pallas_call | solution.py:273
  63.9 1.9 %collective-permute-done.7.refs_1_ = bf16[256,1024]{1,0:T(8,128)(2,1)S(1)} collective-permute-done((bf16[256,1024]{1,0:T(8,128)(2,1)S(1)}, bf16[256,1024]{1,0:T(8,128)(2,1)S(1)}, u32[]{:S(2)}, u32[]{:S(2)}) %collective-permute-start.7) | collective-permute-done | bytes 524320 | tf_op jit(solution)/shard_map/ppermute | solution.py:216
  65.9 8.3 %collective-permute-done.8.refs_2_ = bf16[128,1024]{1,0:T(8,128)(2,1)S(1)} collective-permute-done((bf16[128,1024]{1,0:T(8,128)(2,1)S(1)}, bf16[128,1024]{1,0:T(8,128)(2,1)S(1)}, u32[]{:S(2)}, u32[]{:S(2)}) %collective-permute-start.8) | collective-permute-done | bytes 262176 | tf_op jit(solution)/shard_map/ppermute | solution.py:216
  74.2 1.4 %finish.1 = bf16[128,1024]{1,0:T(8,128)(2,1)} custom-call(f32[256,1024]{1,0:T(8,128)S(1)} %get-tuple-element.15.refs_0_, bf16[256,1024]{1,0:T(8,128)(2,1)S(1)} %collective-permute-done.7.refs_1_, bf16[128,1024]{1,0:T(8,128)(2,1)S(1)} %collective-permute-done.8.refs_2_, bf16[128,1024]{1,0:T(8,128)(2,1)S(1)} %get-tuple-element.17.refs_3_, ...), custom_call_target="tpu_custom_call" | custom-call | tf_op jit(solution)/shard_map/finish/pallas_call | solution.py:289
  (20 shorter events, 0.2 us)
Async XLA Ops:
  0.0 0.7 copy-start.5
  0.7 0.7 copy-start.7
  1.7 0.7 collective-permute-start
  2.4 1.2 %copy-start.1 = (bf16[2048,256]{1,0:T(8,128)(2,1)S(1)}, bf16[2048,256]{1,0:T(8,128)(2,1)}, u32[]{:S(2)}) copy-start(bf16[2048,256]{1,0:T(8,128)(2,1)} %table_ref.3) | copy-start | bytes 3145732
  4.2 14.8 %collective-permute-start.1 = (bf16[128,256]{1,0:T(8,128)(2,1)S(1)}, bf16[128,256]{1,0:T(8,128)(2,1)S(1)}, u32[]{:S(2)}, u32[]{:S(2)}) collective-permute-start(bf16[128,256]{1,0:T(8,128)(2,1)S(1)} %lookup.2), channel_id=1, source_target_pairs={{0,0},{1,5},{2,10},{3,15},{4,4},{5,1},{6,14},{7,11},{8,8},{9,13},{... | collective-permute-start | bytes 196616 | tf_op jit(solution)/shard_map/ppermute | solution.py:216
  4.9 7.6 %collective-permute-start.2 = (s32[1,128]{1,0:T(1,128)S(1)}, s32[1,128]{1,0:T(1,128)S(1)}, u32[]{:S(2)}, u32[]{:S(2)}) collective-permute-start(s32[1,128]{1,0:T(1,128)S(1)} %get-tuple-element.13), channel_id=1, source_target_pairs={{0,28},{1,25},{2,22},{3,19},{4,24},{5,29},{6,18},{7,23},{8,20},{9,... | collective-permute-start | bytes 1544 | tf_op jit(solution)/shard_map/ppermute | solution.py:216
  12.5 1.2 %copy-start.2 = (bf16[2048,256]{1,0:T(8,128)(2,1)S(1)}, bf16[2048,256]{1,0:T(8,128)(2,1)}, u32[]{:S(2)}) copy-start(bf16[2048,256]{1,0:T(8,128)(2,1)} %table_ref.3) | copy-start | bytes 3145732
  14.3 7.1 %collective-permute-start.3 = (bf16[128,256]{1,0:T(8,128)(2,1)S(1)}, bf16[128,256]{1,0:T(8,128)(2,1)S(1)}, u32[]{:S(2)}, u32[]{:S(2)}) collective-permute-start(bf16[128,256]{1,0:T(8,128)(2,1)S(1)} %lookup.3), channel_id=1, source_target_pairs={{0,28},{1,25},{2,22},{3,19},{4,24},{5,29},{6,18},{7,23},{8,20},{9,... | collective-permute-start | bytes 196616 | tf_op jit(solution)/shard_map/ppermute | solution.py:216
  21.4 11.0 %collective-permute-start.4 = (bf16[256,256]{1,0:T(8,128)(2,1)S(1)}, bf16[256,256]{1,0:T(8,128)(2,1)S(1)}, u32[]{:S(2)}, u32[]{:S(2)}) collective-permute-start(bf16[256,256]{1,0:T(8,128)(2,1)S(1)} %constant_dynamic-update-slice_fusion.refs_1_), channel_id=1, source_target_pairs={{0,2},{1,3},{2,0},{3,1},{4,6},{5,7},{6,4},{7,5},{8,10},{9,11},{10,... | collective-permute-start | bytes 393224 | tf_op jit(solution)/shard_map/ppermute | solution.py:216
  29.5 5.0 %collective-permute-start.5 = (bf16[256,256]{1,0:T(8,128)(2,1)S(1)}, bf16[256,256]{1,0:T(8,128)(2,1)S(1)}, u32[]{:S(2)}, u32[]{:S(2)}) collective-permute-start(bf16[256,256]{1,0:T(8,128)(2,1)S(1)} %constant_dynamic-update-slice_fusion.refs_1_), channel_id=1, source_target_pairs={{0,1},{1,0},{2,3},{3,2},{4,5},{5,4},{6,7},{7,6},{8,9},{9,8},{10,11... | collective-permute-start | bytes 393224 | tf_op jit(solution)/shard_map/ppermute | solution.py:216
  32.4 2.1 %collective-permute-start.6 = (bf16[256,256]{1,0:T(8,128)(2,1)S(1)}, bf16[256,256]{1,0:T(8,128)(2,1)S(1)}, u32[]{:S(2)}, u32[]{:S(2)}) collective-permute-start(bf16[256,256]{1,0:T(8,128)(2,1)S(1)} %collective-permute-done.4.refs_2_), channel_id=1, source_target_pairs={{0,1},{1,0},{2,3},{3,2},{4,5},{5,4},{6,7},{7,6},{8,9},{9,8},{10,11... | collective-permute-start | bytes 393224 | tf_op jit(solution)/shard_map/ppermute | solution.py:216
  32.4 0.7 copy-start.6
  34.5 2.2 %copy-start = (bf16[1024,2048]{1,0:T(8,128)(2,1)S(1)}, bf16[1024,2048]{1,0:T(8,128)(2,1)}, u32[]{:S(2)}) copy-start(bf16[1024,2048]{1,0:T(8,128)(2,1)} %refs_6_.1) | copy-start | bytes 12582916
  36.7 1.0 %copy-start.4 = (bf16[256,1024]{1,0:T(8,128)(2,1)S(1)}, bf16[256,1024]{1,0:T(8,128)(2,1)}, u32[]{:S(2)}) copy-start(bf16[256,1024]{1,0:T(8,128)(2,1)} %refs_5_.2) | copy-start | bytes 1572868
  41.0 33.2 %copy-start.3 = (bf16[1024,1024]{1,0:T(8,128)(2,1)S(1)}, bf16[1024,1024]{1,0:T(8,128)(2,1)}, u32[]{:S(2)}) copy-start(bf16[1024,1024]{1,0:T(8,128)(2,1)} %refs_5_.3) | copy-start | bytes 6291460
  63.8 2.0 %collective-permute-start.7 = (bf16[256,1024]{1,0:T(8,128)(2,1)S(1)}, bf16[256,1024]{1,0:T(8,128)(2,1)S(1)}, u32[]{:S(2)}, u32[]{:S(2)}) collective-permute-start(bf16[256,1024]{1,0:T(8,128)(2,1)S(1)} %get-tuple-element.16), channel_id=1, source_target_pairs={{0,1},{1,0},{2,3},{3,2},{4,5},{5,4},{6,7},{7,6},{8,9},{9,8},{10,11... | collective-permute-start | bytes 1572872 | tf_op jit(solution)/shard_map/ppermute | solution.py:216
  65.8 8.4 %collective-permute-start.8 = (bf16[128,1024]{1,0:T(8,128)(2,1)S(1)}, bf16[128,1024]{1,0:T(8,128)(2,1)S(1)}, u32[]{:S(2)}, u32[]{:S(2)}) collective-permute-start(bf16[128,1024]{1,0:T(8,128)(2,1)S(1)} %add_convert_fusion), channel_id=1, source_target_pairs={{0,2},{1,3},{2,0},{3,1},{4,6},{5,7},{6,4},{7,5},{8,10},{9,11},{10,... | collective-permute-start | bytes 786440 | tf_op jit(solution)/shard_map/ppermute | solution.py:216

commit v2 on v1

v2 whole, which is shorter than its diff:
```python
import functools

import jax
import jax.numpy as jnp
from jax import lax
from jax.experimental import pallas as pl
from jax.experimental.pallas import tpu as pltpu
from jax.sharding import PartitionSpec as P

HEADS = 8
KEY_BLOCK = 256
GROUP = 1024
VMEM = pl.BlockSpec(memory_space=pltpu.VMEM)
HBM = pl.BlockSpec(memory_space=pltpu.HBM)
SMEM = pl.BlockSpec(memory_space=pltpu.SMEM)
F32 = jnp.float32
BF16 = jnp.bfloat16
NT = (((1,), (1,)), ((), ()))


def params(mib):
    return pltpu.CompilerParams(vmem_limit_bytes=mib << 20)


def layer_norm(values):
    centre = jnp.mean(values, axis=-1, keepdims=True)
    centred = values - centre
    spread = jnp.mean(centred * centred, axis=-1, keepdims=True)
    return centred * lax.rsqrt(spread + 1e-05)


def silu(values):
    half = values * 0.5
    return half + half * jnp.tanh(half)


def dot(a, b):
    return jnp.dot(a, b, preferred_element_type=F32)


def iota(shape, axis):
    return lax.broadcasted_iota(jnp.int32, shape, axis)


def hi_lo(row):
    wide = jnp.broadcast_to(row, (8, row.shape[1]))
    pick = iota(wide.shape, 0)
    parts = jnp.where(pick == 0, wide >> 8, jnp.where(pick == 1, wide & 255, 0))
    return parts.astype(F32).astype(BF16)


def ranks(packed, per):
    count = packed.shape[1]
    owner_count = lax.axis_size("req")
    codes = (packed >> 16) ^ lax.axis_index("req")
    named = iota((owner_count, count), 0) == codes
    row, column = iota((count, count), 0), iota((count, count), 1)
    earlier = ((row // per == column // per) & (row < column)).astype(F32).astype(BF16)
    before = dot(named.astype(F32).astype(BF16), earlier)
    rank = jnp.sum(jnp.where(named, before, 0.0), axis=0, keepdims=True)
    return codes, rank.astype(jnp.int32)


def code_of(peer, turn, peers):
    return turn * peers + (peer if turn % 2 == 0 else peers - 1 - peer)


def requests_kernel(per, cap, turns, packed_ref, *list_refs):
    peers = lax.axis_size("ctx")
    codes, rank = ranks(packed_ref[...], per)
    place = (iota(codes.shape, 1) // per) * cap + rank
    parts = hi_lo(packed_ref[...] & 65535)
    length = peers * cap
    for turn in range(turns):
        code = code_of(lax.axis_index("ctx"), turn, peers)
        wanted = jnp.where(codes == code, place, -1)
        chosen = (iota((length, codes.shape[1]), 0) == wanted).astype(F32).astype(BF16)
        packed = lax.dot_general(parts, chosen, NT, preferred_element_type=F32)
        packed = packed[0:1] * 256.0 + packed[1:2]
        list_refs[turn][...] = packed.astype(jnp.int32)


def places_kernel(per, cap, turns, packed_ref, places_ref, done_ref):
    peers = lax.axis_size("ctx")
    me = lax.axis_index("ctx")
    codes, rank = ranks(packed_ref[...], per)
    count = codes.shape[1]
    length = peers * cap
    turn = codes // peers
    inner = codes % peers
    peer = jnp.where(turn % 2 == 0, inner, peers - 1 - inner) ^ me
    buffer = jnp.zeros_like(peer)
    for bit, step in enumerate(exchange_steps(peers)):
        buffer = buffer + jnp.where((peer & step) != 0, 1 << bit, 0)
    place = (buffer * turns + turn) * length + (iota(codes.shape, 1) // per) * cap + rank
    row, column = iota((count, count), 0), iota((count, count), 1)
    block = row // per
    half = peers // 2
    relative = jnp.where(block < half, 2 * block, 2 * (block - half) + 1)
    source = (relative ^ me) * per + row % per
    order = (source == column).astype(F32).astype(BF16)
    found = lax.dot_general(order, hi_lo(place), NT, preferred_element_type=F32)
    found = (found[:, 0:1] * 256.0 + found[:, 1:2]).astype(jnp.int32)
    total = places_ref.shape[1]
    places_ref[...] = (iota((count, total), 1) == found).astype(F32).astype(BF16)
    done_ref[...] = jnp.zeros_like(done_ref)


def exchange_steps(peers):
    steps, step = [], peers // 2
    while step >= 1:
        steps.append(step)
        step //= 2
    return steps


def lookup_kernel(turns, table_ref, done_ref, *refs):
    del done_ref
    for list_ref, rows_ref in zip(refs[:turns], refs[turns:]):
        length = list_ref.shape[1]
        same = (iota((length, length), 0) == iota((length, length), 1)).astype(F32).astype(BF16)
        found = lax.dot_general(same, hi_lo(list_ref[...]), NT, preferred_element_type=F32)
        found = (found[:, 0:1] * 256.0 + found[:, 1:2]).astype(jnp.int32)
        chosen = (iota((length, table_ref.shape[0]), 1) == found).astype(F32).astype(BF16)
        rows_ref[...] = dot(chosen, table_ref[...]).astype(BF16)


def attend_kernel(per, buffers, length_ref, places_ref, *refs):
    received, refs = refs[:buffers], refs[buffers:]
    w_in_hbm, w_uq_hbm, keys_hbm, values_hbm = refs[:4]
    features_ref, normed_ref, keep_ref, send_ref = refs[4:8]
    queries_ref, keys_ref, values_ref, w_in_ref, w_query_ref, sems, weight_sems = refs[8:]
    heads, events, head_dim = keys_ref.shape
    width = heads * head_dim
    kept = keep_ref.shape[1]
    scale = 0.5 * head_dim ** (-0.5)
    group = min(GROUP, events)
    block = min(KEY_BLOCK, group)

    def copies(head):
        columns = pl.ds(pl.multiple_of(head * head_dim, head_dim), head_dim)
        return [
            pltpu.make_async_copy(hbm.at[:, columns], ref.at[head], sems.at[index, head])
            for index, (hbm, ref) in enumerate(((keys_hbm, keys_ref), (values_hbm, values_ref)))
        ]

    w_in_copy = pltpu.make_async_copy(w_in_hbm, w_in_ref, weight_sems.at[0])
    w_query_copy = pltpu.make_async_copy(
        w_uq_hbm.at[:, pl.ds(width, width)], w_query_ref, weight_sems.at[1]
    )
    w_in_copy.start()
    w_query_copy.start()

    @pl.loop(0, heads)
    def _(head):
        for copy in copies(head):
            copy.start()

    embedded = None
    start = 0
    for part_ref in received:
        rows = part_ref.shape[0]
        part = dot(places_ref[:, start : start + rows], part_ref[...])
        embedded = part if embedded is None else embedded + part
        start += rows
    w_in_copy.wait()
    features = dot(embedded.astype(BF16), w_in_ref[...]).astype(BF16)
    features_ref[...] = features[:per]
    normed = layer_norm(features.astype(F32)).astype(BF16)
    normed_ref[...] = normed[:per]
    w_query_copy.wait()
    for head in range(heads):
        columns = slice(head * head_dim, (head + 1) * head_dim)
        queries_ref[head] = silu(dot(normed, w_query_ref[:, columns])).astype(BF16)

    valid = length_ref[0] - lax.axis_index("ctx") * events

    def add_group(head, first, total, masked):
        for inner in range(group // block):
            start = first + inner * block
            if not isinstance(start, int):
                start = pl.multiple_of(start, block)
            keys = keys_ref[head, pl.ds(start, block), :]
            values = values_ref[head, pl.ds(start, block), :]
            if masked:
                inside = (iota((block, head_dim), 0) + start) < valid
                values = jnp.where(inside, values.astype(F32), 0.0).astype(BF16)
            half = lax.dot_general(queries_ref[head], keys, NT, preferred_element_type=F32) * scale
            weights = (half + half * jnp.tanh(half)).astype(BF16)
            total = total + dot(weights, values)
        return total

    def store(head, total):
        keep_ref[head] = total[:kept]
        send_ref[head] = total[kept:].astype(BF16)

    zero = jnp.zeros((queries_ref.shape[1], head_dim), F32)

    @pl.when(valid > events - group)
    def _():
        @pl.loop(0, heads)
        def _(head):
            for copy in copies(head):
                copy.wait()
            total = zero
            for first in range(0, events, group):
                total = add_group(head, first, total, first + group >= events)
            store(head, total)

    @pl.when(valid <= events - group)
    def _():
        trips = jnp.maximum(valid + group - 1, 0) // group

        @pl.loop(0, heads)
        def _(head):
            for copy in copies(head):
                copy.wait()
            store(
                head,
                lax.fori_loop(0, trips, lambda i, t: add_group(head, i * group, t, True), zero),
            )


def gate_kernel(normed_ref, w_uq_ref, gate_ref):
    gate_ref[...] = silu(dot(normed_ref[...], w_uq_ref[...])).astype(BF16)


def finish_kernel(others, *refs):
    keep_ref, sibling_ref = refs[:2]
    gate_ref, features_ref, w_out_ref, out_ref = refs[2 + others :]
    parts = []
    for head in range(keep_ref.shape[0]):
        part = keep_ref[head] + sibling_ref[head].astype(F32)
        for other in refs[2 : 2 + others]:
            part = part + other[head].astype(F32)
        parts.append(part)
    attended = jnp.concatenate(parts, axis=1)
    mixed = (layer_norm(attended) * gate_ref[...].astype(F32)).astype(BF16)
    ranked = features_ref[...].astype(F32) + dot(mixed, w_out_ref[...])
    out_ref[...] = ranked.astype(BF16)


def shards(item_table, cand_owner, cand_slot, w_in, w_uq, w_out, k_cache, v_cache, hist_len):
    users, peers = lax.axis_size("req"), lax.axis_size("ctx")
    count = cand_owner.shape[1]
    per = count // peers
    cap = max(2, 2 * per // users)
    turns = users // peers
    length = peers * cap
    width = w_out.shape[0]
    shape = jax.ShapeDtypeStruct

    def permute(values, target):
        pairs = []
        for user in range(users):
            for peer in range(peers):
                to_user, to_peer = target(user, peer)
                pairs.append((user * peers + peer, to_user * peers + to_peer))
        return lax.ppermute(values, ("req", "ctx"), pairs)

    def swap_owner(values, turn):
        return permute(values, lambda user, peer: (user ^ code_of(peer, turn, peers), peer))

    def swap_peer(values, step):
        return permute(values, lambda user, peer: (user, peer ^ step))

    packed = (cand_owner[:, :, 0] << 16) | cand_slot
    lists = pl.pallas_call(
        functools.partial(requests_kernel, per, cap, turns),
        in_specs=[VMEM],
        out_specs=[VMEM] * turns,
        out_shape=[shape((1, length), jnp.int32)] * turns,
        compiler_params=params(16),
        name="requests",
    )(packed)
    asked = [swap_owner(lists[turn], turn) for turn in reversed(range(turns))][::-1]
    places, places_done = pl.pallas_call(
        functools.partial(places_kernel, per, cap, turns),
        in_specs=[VMEM],
        out_specs=[VMEM] * 2,
        out_shape=[shape((count, users * length), BF16), shape((8, 128), jnp.int32)],
        compiler_params=params(16),
        cost_estimate=pl.CostEstimate(flops=1 << 28, bytes_accessed=24 << 20, transcendentals=0),
        name="places",
    )(packed)
    rows = pl.pallas_call(
        functools.partial(lookup_kernel, turns),
        in_specs=[VMEM] * (2 + turns),
        out_specs=[VMEM] * turns,
        out_shape=[shape((length, item_table.shape[1]), BF16)] * turns,
        compiler_params=params(16),
        name="lookup",
    )(item_table, places_done, *asked)
    rows = [swap_owner(rows[turn], turn) for turn in reversed(range(turns))][::-1]
    buffers = [jnp.concatenate(rows, axis=0)]
    for step in exchange_steps(peers):
        buffers = buffers + [swap_peer(one, step) for one in buffers]
    keys, values = k_cache[0], v_cache[0]
    events = keys.shape[0]
    head_dim = width // HEADS
    half = count // 2
    features, normed, keep, send = pl.pallas_call(
        functools.partial(attend_kernel, per, len(buffers)),
        in_specs=[SMEM] + [VMEM] * (1 + len(buffers)) + [HBM] * 4,
        out_specs=[VMEM] * 4,
        out_shape=[
            shape((per, width), BF16),
            shape((per, width), BF16),
            shape((HEADS, half, head_dim), F32),
            shape((HEADS, half, head_dim), BF16),
        ],
        scratch_shapes=[
            pltpu.VMEM((HEADS, count, head_dim), BF16),
            pltpu.VMEM((HEADS, events, head_dim), BF16),
            pltpu.VMEM((HEADS, events, head_dim), BF16),
            pltpu.VMEM(w_in.shape, BF16),
            pltpu.VMEM((width, width), BF16),
            pltpu.SemaphoreType.DMA((2, HEADS)),
            pltpu.SemaphoreType.DMA((2,)),
        ],
        compiler_params=params(47),
        name="attend",
    )(hist_len, places, *buffers, w_in, w_uq, keys, values)
    gate = pl.pallas_call(
        gate_kernel,
        grid=(1,),
        in_specs=[
            pl.BlockSpec((per, width), lambda i: (0, 0)),
            pl.BlockSpec((width, width), lambda i: (0, 0)),
        ],
        out_specs=pl.BlockSpec((per, width), lambda i: (0, 0)),
        out_shape=shape((per, width), BF16),
        compiler_params=params(16),
        cost_estimate=pl.CostEstimate(flops=1 << 28, bytes_accessed=3 << 20, transcendentals=0),
        name="gate",
    )(normed, w_uq)
    sibling = swap_peer(send, 1)
    others = []
    for index in range(1, peers // 2):
        piece = slice(index * per, (index + 1) * per)
        summed = (keep[:, piece] + sibling[:, piece].astype(F32)).astype(BF16)
        others.append(swap_peer(summed, 2 * index))
    block = pl.BlockSpec((HEADS, per, head_dim), lambda i: (0, 0, 0))
    ranked = pl.pallas_call(
        functools.partial(finish_kernel, len(others)),
        grid=(1,),
        in_specs=[block] * (2 + len(others))
        + [pl.BlockSpec((per, width), lambda i: (0, 0))] * 2
        + [pl.BlockSpec((width, width), lambda i: (0, 0))],
        out_specs=pl.BlockSpec((per, width), lambda i: (0, 0)),
        out_shape=shape((per, width), BF16),
        compiler_params=params(24),
        name="finish",
    )(keep, sibling, *others, gate, features, w_out)
    return ranked[None]


def solution(mesh):
    in_specs = (
        P("req", None),
        P("req", None, None),
        P("req", None),
        P(),
        P(),
        P(),
        P("req", "ctx", None),
        P("req", "ctx", None),
        P("req"),
    )
    out_specs = P("req", "ctx", None)
    return jax.shard_map(shards, mesh=mesh, in_specs=in_specs, out_specs=out_specs, check_vma=False)
```

time: 76.6 us -> 65.9 us (0.86); the launches traced: 75.6 us -> 65.7 us
  local copies, waits for them, and re-layouts: 7.73 us -> 2.28 us
  starting transfers between devices: 20.4 us -> 16.6 us
  Pallas kernels: 29.6 us -> 28.8 us
    unnamed x17 -> x9, local copies, waits for them, and re-layouts: 7.72 us -> 2.28 us
    ppermute x9, starting transfers between devices: 20.4 us -> 16.6 us  [permute(): return lax.ppermute(values, ('req', 'ctx'), pairs)]
    pallas_call x4 -> x3, Pallas kernels: 27.2 us -> 26.3 us  [the longest x1 25.2 us: shards(): pl.pallas_call(functools.partial(attend_kernel, per, len(buffers)), in_sp...]
  transfers between devices with their start and end apart: 9 -> 9, of which waited for: 5 -> 6; matrix products, arithmetic and copies ran while one was open for 0% -> 0% of each run, Pallas kernels for 2% -> 2%
where the time goes in v2:
time: 65.9 us; the launch traced here: 65.7 us
  Pallas kernels  28.8 us (44%)
  starting transfers between devices  16.6 us (25%)
  waiting for transfers between devices  16.5 us (25%)
  local copies, waits for them, and re-layouts  2.28 us (3%)
  other arithmetic  0.76 us (1%)
  between operations  0.76 us (1%)
    pallas_call x1, Pallas kernels, shards(): pl.pallas_call(functools.partial(attend_kernel, per, len(buffers)), in_sp...  25.2 us
    ppermute x9, starting transfers between devices, permute(): return lax.ppermute(values, ('req', 'ctx'), pairs)  16.6 us
    ppermute x9, waiting for transfers between devices, permute(): return lax.ppermute(values, ('req', 'ctx'), pairs)  16.5 us
    unnamed x9, local copies, waits for them, and re-layouts  2.28 us
    pallas_call x1, Pallas kernels, shards(): pl.pallas_call(functools.partial(finish_kernel, len(others)), grid=(1,),...  1.37 us
  transfers between devices with their start and end apart: 9, of which 6 were waited for; matrix products, arithmetic and copies ran while one was open for 0% of the time, Pallas kernels for 2%

profile of v2, /device:TPU:0, one launch (start us, length us, event | category | flops | bytes accessed | tf_op | source)
XLA Modules:
  0.0 65.7 jit_solution(4507136744031675287)
XLA Ops:
  0.0 0.7 %bitcast_or_fusion.packed_ref = s32[1,512]{1,0:T(1,128)S(1)} fusion(s32[1,512]{1,0:T(1,128)} %param.11, s32[1,512,1]{1,2,0:T(1,128)} %param.10), kind=kLoop, calls=%fused_computation.3 | loop fusion | flops 1024 | bytes 6144 | tf_op jit(solution)/shard_map/or | solution.py:267
  0.7 0.4 requests.1
  1.1 0.7 %collective-permute-start = (s32[1,128]{1,0:T(1,128)S(1)}, s32[1,128]{1,0:T(1,128)S(1)}, u32[]{:S(2)}, u32[]{:S(2)}) collective-permute-start(s32[1,128]{1,0:T(1,128)S(1)} %get-tuple-element.17), channel_id=1, source_target_pairs={{0,0},{1,5},{2,10},{3,15},{4,4},{5,1},{6,14},{7,11},{8,8},{9,13},{... | collective-permute-start | bytes 1544 | tf_op jit(solution)/shard_map/ppermute | solution.py:259
  1.7 6.0 %collective-permute-start.1 = (s32[1,128]{1,0:T(1,128)S(1)}, s32[1,128]{1,0:T(1,128)S(1)}, u32[]{:S(2)}, u32[]{:S(2)}) collective-permute-start(s32[1,128]{1,0:T(1,128)S(1)} %get-tuple-element.18), channel_id=1, source_target_pairs={{0,28},{1,25},{2,22},{3,19},{4,24},{5,29},{6,18},{7,23},{8,20},{9,... | collective-permute-start | bytes 1544 | tf_op jit(solution)/shard_map/ppermute | solution.py:259
  7.8 0.7 %places.1 = (bf16[512,1024]{1,0:T(8,128)(2,1)S(1)}, s32[8,128]{1,0:T(8,128)S(1)}) custom-call(s32[1,512]{1,0:T(1,128)S(1)} %bitcast_or_fusion.packed_ref), custom_call_target="tpu_custom_call" | custom-call | flops 268435456 | bytes 25165824 | tf_op jit(solution)/shard_map/places/pallas_call | solution.py:277
  8.5 0.0 collective-permute-done.refs_0_
  8.5 0.8 %collective-permute-done.1.refs_1_ = s32[1,128]{1,0:T(1,128)S(1)} collective-permute-done((s32[1,128]{1,0:T(1,128)S(1)}, s32[1,128]{1,0:T(1,128)S(1)}, u32[]{:S(2)}, u32[]{:S(2)}) %collective-permute-start.1) | collective-permute-done | bytes 544 | tf_op jit(solution)/shard_map/ppermute | solution.py:259
  9.3 1.2 %copy-done.2 = bf16[2048,256]{1,0:T(8,128)(2,1)S(1)} copy-done((bf16[2048,256]{1,0:T(8,128)(2,1)S(1)}, bf16[2048,256]{1,0:T(8,128)(2,1)}, u32[]{:S(2)}) %copy-start.2) | copy-done | bytes 1048600
  10.5 0.7 %lookup.1 = (bf16[128,256]{1,0:T(8,128)(2,1)S(1)}, bf16[128,256]{1,0:T(8,128)(2,1)S(1)}) custom-call(bf16[2048,256]{1,0:T(8,128)(2,1)S(1)} %copy-done.2, s32[8,128]{1,0:T(8,128)S(1)} %get-tuple-element.16.done_ref, s32[1,128]{1,0:T(1,128)S(1)} %collective-permute-done.refs_0_, s32[1,128]{1,0:T(1,128)S(1)} %collective-permute-done.1.refs_1_), custom_call_target="tpu_custom_call" | custom-call | tf_op jit(solution)/shard_map/lookup/pallas_call | solution.py:286
  11.2 0.7 %collective-permute-start.2 = (bf16[128,256]{1,0:T(8,128)(2,1)S(1)}, bf16[128,256]{1,0:T(8,128)(2,1)S(1)}, u32[]{:S(2)}, u32[]{:S(2)}) collective-permute-start(bf16[128,256]{1,0:T(8,128)(2,1)S(1)} %get-tuple-element.19), channel_id=1, source_target_pairs={{0,0},{1,5},{2,10},{3,15},{4,4},{5,1},{6,14},{7,11},{8,8},{9,13},{... | collective-permute-start | bytes 196616 | tf_op jit(solution)/shard_map/ppermute | solution.py:259
  11.9 4.8 %collective-permute-start.3 = (bf16[128,256]{1,0:T(8,128)(2,1)S(1)}, bf16[128,256]{1,0:T(8,128)(2,1)S(1)}, u32[]{:S(2)}, u32[]{:S(2)}) collective-permute-start(bf16[128,256]{1,0:T(8,128)(2,1)S(1)} %get-tuple-element.20), channel_id=1, source_target_pairs={{0,28},{1,25},{2,22},{3,19},{4,24},{5,29},{6,18},{7,23},{8,20},{9,... | collective-permute-start | bytes 196616 | tf_op jit(solution)/shard_map/ppermute | solution.py:259
  16.7 2.3 %collective-permute-done.3 = bf16[128,256]{1,0:T(8,128)(2,1)S(1)} collective-permute-done((bf16[128,256]{1,0:T(8,128)(2,1)S(1)}, bf16[128,256]{1,0:T(8,128)(2,1)S(1)}, u32[]{:S(2)}, u32[]{:S(2)}) %collective-permute-start.3) | collective-permute-done | bytes 65568 | tf_op jit(solution)/shard_map/ppermute | solution.py:259
  19.0 4.3 %collective-permute-start.4 = (bf16[256,256]{1,0:T(8,128)(2,1)S(1)}, bf16[256,256]{1,0:T(8,128)(2,1)S(1)}, u32[]{:S(2)}, u32[]{:S(2)}) collective-permute-start(bf16[256,256]{1,0:T(8,128)(2,1)S(1)} %constant_dynamic-update-slice_fusion.refs_0_), channel_id=1, source_target_pairs={{0,2},{1,3},{2,0},{3,1},{4,6},{5,7},{6,4},{7,5},{8,10},{9,11},{10,... | collective-permute-start | bytes 393224 | tf_op jit(solution)/shard_map/ppermute | solution.py:259
  23.4 2.9 %collective-permute-done.4.refs_1_ = bf16[256,256]{1,0:T(8,128)(2,1)S(1)} collective-permute-done((bf16[256,256]{1,0:T(8,128)(2,1)S(1)}, bf16[256,256]{1,0:T(8,128)(2,1)S(1)}, u32[]{:S(2)}, u32[]{:S(2)}) %collective-permute-start.4) | collective-permute-done | bytes 131104 | tf_op jit(solution)/shard_map/ppermute | solution.py:259
  27.0 0.7 %collective-permute-done.6.refs_3_ = bf16[256,256]{1,0:T(8,128)(2,1)S(1)} collective-permute-done((bf16[256,256]{1,0:T(8,128)(2,1)S(1)}, bf16[256,256]{1,0:T(8,128)(2,1)S(1)}, u32[]{:S(2)}, u32[]{:S(2)}) %collective-permute-start.6) | collective-permute-done | bytes 131104 | tf_op jit(solution)/shard_map/ppermute | solution.py:259
  27.6 1.0 %copy-done.3 = bf16[256,1024]{1,0:T(8,128)(2,1)S(1)} copy-done((bf16[256,1024]{1,0:T(8,128)(2,1)S(1)}, bf16[256,1024]{1,0:T(8,128)(2,1)}, u32[]{:S(2)}) %copy-start.3) | copy-done | bytes 524312
  28.7 25.2 %attend.1 = (bf16[128,1024]{1,0:T(8,128)(2,1)S(1)}, bf16[128,1024]{1,0:T(8,128)(2,1)S(1)}, f32[8,256,128]{2,1,0:T(8,128)S(1)}, bf16[8,256,128]{2,1,0:T(8,128)(2,1)S(1)}) custom-call(s32[1]{0:T(128)S(6)} %copy.11.length_ref, bf16[512,1024]{1,0:T(8,128)(2,1)S(1)} %get-tuple-element.15.places_ref, ...), custom_call_target="tpu_custom_call" | custom-call | tf_op jit(solution)/shard_map/attend/pallas_call | solution.py:302
  53.9 0.1 collective-permute-start.7
  53.9 1.9 %collective-permute-done.7.refs_1_ = bf16[8,256,128]{2,1,0:T(8,128)(2,1)S(1)} collective-permute-done((bf16[8,256,128]{2,1,0:T(8,128)(2,1)S(1)}, bf16[8,256,128]{2,1,0:T(8,128)(2,1)S(1)}, u32[]{:S(2)}, u32[]{:S(2)}) %collective-permute-start.7) | collective-permute-done | bytes 524320 | tf_op jit(solution)/shard_map/ppermute | solution.py:259
  55.8 0.1 add_convert_fusion
  55.9 0.1 collective-permute-start.8
  56.0 0.5 gate.1.refs_3_
  56.5 7.8 %collective-permute-done.8.refs_2_ = bf16[8,128,128]{2,1,0:T(8,128)(2,1)S(1)} collective-permute-done((bf16[8,128,128]{2,1,0:T(8,128)(2,1)S(1)}, bf16[8,128,128]{2,1,0:T(8,128)(2,1)S(1)}, u32[]{:S(2)}, u32[]{:S(2)}) %collective-permute-start.8) | collective-permute-done | bytes 262176 | tf_op jit(solution)/shard_map/ppermute | solution.py:259
  64.3 1.4 %finish.1 = bf16[128,1024]{1,0:T(8,128)(2,1)} custom-call(f32[8,256,128]{2,1,0:T(8,128)S(1)} %get-tuple-element.21.refs_0_, bf16[8,256,128]{2,1,0:T(8,128)(2,1)S(1)} %collective-permute-done.7.refs_1_, bf16[8,128,128]{2,1,0:T(8,128)(2,1)S(1)} %collective-permute-done.8.refs_2_, bf16[128,1024]{1,0:T(8,128)(2,1)S(1)} %gate.1.refs_3_, ...), custom_call_target="tpu_custom_call" | custom-call | tf_op jit(solution)/shard_map/finish/pallas_call | solution.py:344
  (12 shorter events, 0.0 us)
Async XLA Ops:
  1.1 7.4 %collective-permute-start = (s32[1,128]{1,0:T(1,128)S(1)}, s32[1,128]{1,0:T(1,128)S(1)}, u32[]{:S(2)}, u32[]{:S(2)}) collective-permute-start(s32[1,128]{1,0:T(1,128)S(1)} %get-tuple-element.17), channel_id=1, source_target_pairs={{0,0},{1,5},{2,10},{3,15},{4,4},{5,1},{6,14},{7,11},{8,8},{9,13},{... | collective-permute-start | bytes 1544 | tf_op jit(solution)/shard_map/ppermute | solution.py:259
  1.7 7.6 %collective-permute-start.1 = (s32[1,128]{1,0:T(1,128)S(1)}, s32[1,128]{1,0:T(1,128)S(1)}, u32[]{:S(2)}, u32[]{:S(2)}) collective-permute-start(s32[1,128]{1,0:T(1,128)S(1)} %get-tuple-element.18), channel_id=1, source_target_pairs={{0,28},{1,25},{2,22},{3,19},{4,24},{5,29},{6,18},{7,23},{8,20},{9,... | collective-permute-start | bytes 1544 | tf_op jit(solution)/shard_map/ppermute | solution.py:259
  9.3 1.2 %copy-start.2 = (bf16[2048,256]{1,0:T(8,128)(2,1)S(1)}, bf16[2048,256]{1,0:T(8,128)(2,1)}, u32[]{:S(2)}) copy-start(bf16[2048,256]{1,0:T(8,128)(2,1)} %table_ref.1) | copy-start | bytes 3145732
  11.2 5.5 %collective-permute-start.2 = (bf16[128,256]{1,0:T(8,128)(2,1)S(1)}, bf16[128,256]{1,0:T(8,128)(2,1)S(1)}, u32[]{:S(2)}, u32[]{:S(2)}) collective-permute-start(bf16[128,256]{1,0:T(8,128)(2,1)S(1)} %get-tuple-element.19), channel_id=1, source_target_pairs={{0,0},{1,5},{2,10},{3,15},{4,4},{5,1},{6,14},{7,11},{8,8},{9,13},{... | collective-permute-start | bytes 196616 | tf_op jit(solution)/shard_map/ppermute | solution.py:259
  11.9 7.1 %collective-permute-start.3 = (bf16[128,256]{1,0:T(8,128)(2,1)S(1)}, bf16[128,256]{1,0:T(8,128)(2,1)S(1)}, u32[]{:S(2)}, u32[]{:S(2)}) collective-permute-start(bf16[128,256]{1,0:T(8,128)(2,1)S(1)} %get-tuple-element.20), channel_id=1, source_target_pairs={{0,28},{1,25},{2,22},{3,19},{4,24},{5,29},{6,18},{7,23},{8,20},{9,... | collective-permute-start | bytes 196616 | tf_op jit(solution)/shard_map/ppermute | solution.py:259
  19.0 7.3 %collective-permute-start.4 = (bf16[256,256]{1,0:T(8,128)(2,1)S(1)}, bf16[256,256]{1,0:T(8,128)(2,1)S(1)}, u32[]{:S(2)}, u32[]{:S(2)}) collective-permute-start(bf16[256,256]{1,0:T(8,128)(2,1)S(1)} %constant_dynamic-update-slice_fusion.refs_0_), channel_id=1, source_target_pairs={{0,2},{1,3},{2,0},{3,1},{4,6},{5,7},{6,4},{7,5},{8,10},{9,11},{10,... | collective-permute-start | bytes 393224 | tf_op jit(solution)/shard_map/ppermute | solution.py:259
  23.3 3.6 %collective-permute-start.5 = (bf16[256,256]{1,0:T(8,128)(2,1)S(1)}, bf16[256,256]{1,0:T(8,128)(2,1)S(1)}, u32[]{:S(2)}, u32[]{:S(2)}) collective-permute-start(bf16[256,256]{1,0:T(8,128)(2,1)S(1)} %constant_dynamic-update-slice_fusion.refs_0_), channel_id=1, source_target_pairs={{0,1},{1,0},{2,3},{3,2},{4,5},{5,4},{6,7},{7,6},{8,9},{9,8},{10,11... | collective-permute-start | bytes 393224 | tf_op jit(solution)/shard_map/ppermute | solution.py:259
  26.3 1.3 %collective-permute-start.6 = (bf16[256,256]{1,0:T(8,128)(2,1)S(1)}, bf16[256,256]{1,0:T(8,128)(2,1)S(1)}, u32[]{:S(2)}, u32[]{:S(2)}) collective-permute-start(bf16[256,256]{1,0:T(8,128)(2,1)S(1)} %collective-permute-done.4.refs_1_), channel_id=1, source_target_pairs={{0,1},{1,0},{2,3},{3,2},{4,5},{5,4},{6,7},{7,6},{8,9},{9,8},{10,11... | collective-permute-start | bytes 393224 | tf_op jit(solution)/shard_map/ppermute | solution.py:259
  27.6 1.0 %copy-start.3 = (bf16[256,1024]{1,0:T(8,128)(2,1)S(1)}, bf16[256,1024]{1,0:T(8,128)(2,1)}, u32[]{:S(2)}) copy-start(bf16[256,1024]{1,0:T(8,128)(2,1)} %refs_4_.1) | copy-start | bytes 1572868
  28.7 27.3 %copy-start = (bf16[1024,2048]{1,0:T(8,128)(2,1)S(1)}, bf16[1024,2048]{1,0:T(8,128)(2,1)}, u32[]{:S(2)}) copy-start(bf16[1024,2048]{1,0:T(8,128)(2,1)} %w_uq_ref.1) | copy-start | bytes 12582916
  28.7 35.6 %copy-start.1 = (bf16[1024,1024]{1,0:T(8,128)(2,1)S(1)}, bf16[1024,1024]{1,0:T(8,128)(2,1)}, u32[]{:S(2)}) copy-start(bf16[1024,1024]{1,0:T(8,128)(2,1)} %refs_5_.3) | copy-start | bytes 6291460
  53.9 2.0 %collective-permute-start.7 = (bf16[8,256,128]{2,1,0:T(8,128)(2,1)S(1)}, bf16[8,256,128]{2,1,0:T(8,128)(2,1)S(1)}, u32[]{:S(2)}, u32[]{:S(2)}) collective-permute-start(bf16[8,256,128]{2,1,0:T(8,128)(2,1)S(1)} %get-tuple-element.22), channel_id=1, source_target_pairs={{0,1},{1,0},{2,3},{3,2},{4,5},{5,4},{6,7},{7,6},{8,9},{9,8},{10,11... | collective-permute-start | bytes 1572872 | tf_op jit(solution)/shard_map/ppermute | solution.py:259
  55.9 8.4 %collective-permute-start.8 = (bf16[8,128,128]{2,1,0:T(8,128)(2,1)S(1)}, bf16[8,128,128]{2,1,0:T(8,128)(2,1)S(1)}, u32[]{:S(2)}, u32[]{:S(2)}) collective-permute-start(bf16[8,128,128]{2,1,0:T(8,128)(2,1)S(1)} %add_convert_fusion), channel_id=1, source_target_pairs={{0,2},{1,3},{2,0},{3,1},{4,6},{5,7},{6,4},{7,5},{8,10},{9,11},{10,... | collective-permute-start | bytes 786440 | tf_op jit(solution)/shard_map/ppermute | solution.py:259

commit v3 on v2

--- a/solution.py
+++ b/solution.py
@@ -52,7 +52,7 @@
 def ranks(packed, per):
     count = packed.shape[1]
     owner_count = lax.axis_size("req")
-    codes = (packed >> 16) ^ lax.axis_index("req")
+    codes = (packed >> 16) ^ lax.axis_index("req") ^ (owner_count - 1)
     named = iota((owner_count, count), 0) == codes
     row, column = iota((count, count), 0), iota((count, count), 1)
     earlier = ((row // per == column // per) & (row < column)).astype(F32).astype(BF16)
@@ -80,7 +80,9 @@
         list_refs[turn][...] = packed.astype(jnp.int32)
 
 
-def places_kernel(per, cap, turns, packed_ref, places_ref, done_ref):
+def places_kernel(per, cap, turns, packed_ref, table_ref, w_in_ref, places_ref, *held):
+    held[0][...] = table_ref[...]
+    held[1][...] = w_in_ref[...]
     peers = lax.axis_size("ctx")
     me = lax.axis_index("ctx")
     codes, rank = ranks(packed_ref[...], per)
@@ -103,7 +105,6 @@
     found = (found[:, 0:1] * 256.0 + found[:, 1:2]).astype(jnp.int32)
     total = places_ref.shape[1]
     places_ref[...] = (iota((count, total), 1) == found).astype(F32).astype(BF16)
-    done_ref[...] = jnp.zeros_like(done_ref)
 
 
 def exchange_steps(peers):
@@ -114,8 +115,7 @@
     return steps
 
 
-def lookup_kernel(turns, table_ref, done_ref, *refs):
-    del done_ref
+def lookup_kernel(turns, table_ref, *refs):
     for list_ref, rows_ref in zip(refs[:turns], refs[turns:]):
         length = list_ref.shape[1]
         same = (iota((length, length), 0) == iota((length, length), 1)).astype(F32).astype(BF16)
@@ -127,9 +127,9 @@
 
 def attend_kernel(per, buffers, length_ref, places_ref, *refs):
     received, refs = refs[:buffers], refs[buffers:]
-    w_in_hbm, w_uq_hbm, keys_hbm, values_hbm = refs[:4]
+    w_in_ref, w_uq_hbm, keys_hbm, values_hbm = refs[:4]
     features_ref, normed_ref, keep_ref, send_ref = refs[4:8]
-    queries_ref, keys_ref, values_ref, w_in_ref, w_query_ref, sems, weight_sems = refs[8:]
+    queries_ref, keys_ref, values_ref, w_query_ref, sems, weight_sem = refs[8:]
     heads, events, head_dim = keys_ref.shape
     width = heads * head_dim
     kept = keep_ref.shape[1]
@@ -144,11 +144,9 @@
             for index, (hbm, ref) in enumerate(((keys_hbm, keys_ref), (values_hbm, values_ref)))
         ]
 
-    w_in_copy = pltpu.make_async_copy(w_in_hbm, w_in_ref, weight_sems.at[0])
     w_query_copy = pltpu.make_async_copy(
-        w_uq_hbm.at[:, pl.ds(width, width)], w_query_ref, weight_sems.at[1]
+        w_uq_hbm.at[:, pl.ds(width, width)], w_query_ref, weight_sem
     )
-    w_in_copy.start()
     w_query_copy.start()
 
     @pl.loop(0, heads)
@@ -163,31 +161,45 @@
         part = dot(places_ref[:, start : start + rows], part_ref[...])
         embedded = part if embedded is None else embedded + part
         start += rows
-    w_in_copy.wait()
     features = dot(embedded.astype(BF16), w_in_ref[...]).astype(BF16)
     features_ref[...] = features[:per]
     normed = layer_norm(features.astype(F32)).astype(BF16)
     normed_ref[...] = normed[:per]
     w_query_copy.wait()
-    for head in range(heads):
-        columns = slice(head * head_dim, (head + 1) * head_dim)
-        queries_ref[head] = silu(dot(normed, w_query_ref[:, columns])).astype(BF16)
+    together = 4
+    for first in range(0, heads, together):
+        columns = slice(first * head_dim, (first + together) * head_dim)
+        queries = silu(dot(normed, w_query_ref[:, columns])).astype(BF16)
+        for index in range(together):
+            part = slice(index * head_dim, (index + 1) * head_dim)
+            queries_ref[first + index] = queries[:, part]
 
     valid = length_ref[0] - lax.axis_index("ctx") * events
 
     def add_group(head, first, total, masked):
+        def weights_of(start):
+            keys = keys_ref[head, pl.ds(start, block), :]
+            half = lax.dot_general(queries_ref[head], keys, NT, preferred_element_type=F32) * scale
+            return (half + half * jnp.tanh(half)).astype(BF16)
+
+        def values_of(start):
+            values = values_ref[head, pl.ds(start, block), :]
+            if masked:
+                inside = (iota((block, head_dim), 0) + start) < valid
+                values = jnp.where(inside, values.astype(F32), 0.0).astype(BF16)
+            return values
+
+        waiting = []
         for inner in range(group // block):
             start = first + inner * block
             if not isinstance(start, int):
                 start = pl.multiple_of(start, block)
-            keys = keys_ref[head, pl.ds(start, block), :]
-            values = values_ref[head, pl.ds(start, block), :]
-            if masked:
-                inside = (iota((block, head_dim), 0) + start) < valid
-                values = jnp.where(inside, values.astype(F32), 0.0).astype(BF16)
-            half = lax.dot_general(queries_ref[head], keys, NT, preferred_element_type=F32) * scale
-            weights = (half + half * jnp.tanh(half)).astype(BF16)
-            total = total + dot(weights, values)
+            waiting.append((weights_of(start), start))
+            if len(waiting) > 0:
+                weights, before = waiting.pop(0)
+                total = total + dot(weights, values_of(before))
+        for weights, before in waiting:
+            total = total + dot(weights, values_of(before))
         return total
 
     def store(head, total):
@@ -198,14 +210,16 @@
 
     @pl.when(valid > events - group)
     def _():
-        @pl.loop(0, heads)
+        @pl.loop(0, heads // 4)
         def _(head):
-            for copy in copies(head):
-                copy.wait()
-            total = zero
-            for first in range(0, events, group):
-                total = add_group(head, first, total, first + group >= events)
-            store(head, total)
+            for one in [4 * head + extra for extra in range(4)]:
+                for copy in copies(one):
+                    copy.wait()
+            for one in [4 * head + extra for extra in range(4)]:
+                total = zero
+                for first in range(0, events, group):
+                    total = add_group(one, first, total, first + group >= events)
+                store(one, total)
 
     @pl.when(valid <= events - group)
     def _():
@@ -259,7 +273,7 @@
         return lax.ppermute(values, ("req", "ctx"), pairs)
 
     def swap_owner(values, turn):
-        return permute(values, lambda user, peer: (user ^ code_of(peer, turn, peers), peer))
+        return permute(values, lambda user, peer: (user ^ (users - 1) ^ code_of(peer, turn, peers), peer))
 
     def swap_peer(values, step):
         return permute(values, lambda user, peer: (user, peer ^ step))
@@ -274,23 +288,23 @@
         name="requests",
     )(packed)
     asked = [swap_owner(lists[turn], turn) for turn in reversed(range(turns))][::-1]
-    places, places_done = pl.pallas_call(
+    places, table, w_in = pl.pallas_call(
         functools.partial(places_kernel, per, cap, turns),
-        in_specs=[VMEM],
-        out_specs=[VMEM] * 2,
-        out_shape=[shape((count, users * length), BF16), shape((8, 128), jnp.int32)],
+        in_specs=[VMEM] * 3,
+        out_specs=[VMEM] * 3,
+        out_shape=[shape((count, users * length), BF16), shape(item_table.shape, BF16), shape(w_in.shape, BF16)],
         compiler_params=params(16),
         cost_estimate=pl.CostEstimate(flops=1 << 28, bytes_accessed=24 << 20, transcendentals=0),
         name="places",
-    )(packed)
+    )(packed, item_table, w_in)
     rows = pl.pallas_call(
         functools.partial(lookup_kernel, turns),
-        in_specs=[VMEM] * (2 + turns),
+        in_specs=[VMEM] * (1 + turns),
         out_specs=[VMEM] * turns,
         out_shape=[shape((length, item_table.shape[1]), BF16)] * turns,
         compiler_params=params(16),
         name="lookup",
-    )(item_table, places_done, *asked)
+    )(table, *asked)
     rows = [swap_owner(rows[turn], turn) for turn in reversed(range(turns))][::-1]
     buffers = [jnp.concatenate(rows, axis=0)]
     for step in exchange_steps(peers):
@@ -301,7 +315,7 @@
     half = count // 2
     features, normed, keep, send = pl.pallas_call(
         functools.partial(attend_kernel, per, len(buffers)),
-        in_specs=[SMEM] + [VMEM] * (1 + len(buffers)) + [HBM] * 4,
+        in_specs=[SMEM] + [VMEM] * (1 + len(buffers)) + [VMEM] + [HBM] * 3,
         out_specs=[VMEM] * 4,
         out_shape=[
             shape((per, width), BF16),
@@ -313,10 +327,9 @@
             pltpu.VMEM((HEADS, count, head_dim), BF16),
             pltpu.VMEM((HEADS, events, head_dim), BF16),
             pltpu.VMEM((HEADS, events, head_dim), BF16),
-            pltpu.VMEM(w_in.shape, BF16),
             pltpu.VMEM((width, width), BF16),
             pltpu.SemaphoreType.DMA((2, HEADS)),
-            pltpu.SemaphoreType.DMA((2,)),
+            pltpu.SemaphoreType.DMA,
         ],
         compiler_params=params(47),
         name="attend",

time: 65.9 us -> 61.2 us (0.929)
  starting transfers between devices: 16.6 us -> 13.1 us
  Pallas kernels: 28.8 us -> 26.4 us
  waiting for transfers between devices: 16.5 us -> 17.2 us
    ppermute x9, starting transfers between devices: 16.6 us -> 13.1 us  [permute(): return lax.ppermute(values, ('req', 'ctx'), pairs)]
    pallas_call x1, Pallas kernels: 25.2 us -> 22.7 us  [shards(): pl.pallas_call(functools.partial(attend_kernel, per, len(buffers)), in_sp...]
    ppermute x9, waiting for transfers between devices: 16.5 us -> 17.2 us  [permute(): return lax.ppermute(values, ('req', 'ctx'), pairs)]
  transfers between devices with their start and end apart: 9 -> 9, of which waited for: 6 -> 5; matrix products, arithmetic and copies ran while one was open for 0% -> 0% of each run, Pallas kernels for 2% -> 2%
where the time goes in v3:
time: 61.2 us; the launch traced here: 60.5 us
  Pallas kernels  26.4 us (43%)
  waiting for transfers between devices  17.2 us (28%)
  starting transfers between devices  13.1 us (21%)
  local copies, waits for them, and re-layouts  2.28 us (4%)
  between operations  0.78 us (1%)
  other arithmetic  0.76 us (1%)
    pallas_call x1, Pallas kernels, shards(): pl.pallas_call(functools.partial(attend_kernel, per, len(buffers)), in_sp...  22.7 us
    ppermute x9, waiting for transfers between devices, permute(): return lax.ppermute(values, ('req', 'ctx'), pairs)  17.2 us
    ppermute x9, starting transfers between devices, permute(): return lax.ppermute(values, ('req', 'ctx'), pairs)  13.1 us
    unnamed x9, local copies, waits for them, and re-layouts  2.27 us
    pallas_call x1, Pallas kernels, shards(): pl.pallas_call(functools.partial(finish_kernel, len(others)), grid=(1,),...  1.36 us
  transfers between devices with their start and end apart: 9, of which 5 were waited for; matrix products, arithmetic and copies ran while one was open for 0% of the time, Pallas kernels for 2%

profile of v3, /device:TPU:0, one launch (start us, length us, event | category | flops | bytes accessed | tf_op | source)
XLA Modules:
  0.0 60.5 jit_solution(795748249596510857)
XLA Ops:
  0.0 0.7 %bitcast_or_fusion.packed_ref = s32[1,512]{1,0:T(1,128)S(1)} fusion(s32[1,512]{1,0:T(1,128)} %param.11, s32[1,512,1]{1,2,0:T(1,128)} %param.10), kind=kLoop, calls=%fused_computation.3 | loop fusion | flops 1024 | bytes 6144 | tf_op jit(solution)/shard_map/or | solution.py:281
  0.7 0.4 requests.1
  1.1 6.0 %collective-permute-start = (s32[1,128]{1,0:T(1,128)S(1)}, s32[1,128]{1,0:T(1,128)S(1)}, u32[]{:S(2)}, u32[]{:S(2)}) collective-permute-start(s32[1,128]{1,0:T(1,128)S(1)} %get-tuple-element.18), channel_id=1, source_target_pairs={{0,28},{1,25},{2,22},{3,19},{4,24},{5,29},{6,18},{7,23},{8,20},{9,... | collective-permute-start | bytes 1544 | tf_op jit(solution)/shard_map/ppermute | solution.py:273
  7.1 0.6 %collective-permute-start.1 = (s32[1,128]{1,0:T(1,128)S(1)}, s32[1,128]{1,0:T(1,128)S(1)}, u32[]{:S(2)}, u32[]{:S(2)}) collective-permute-start(s32[1,128]{1,0:T(1,128)S(1)} %get-tuple-element.19), channel_id=1, source_target_pairs={{0,0},{1,5},{2,10},{3,15},{4,4},{5,1},{6,14},{7,11},{8,8},{9,13},{... | collective-permute-start | bytes 1544 | tf_op jit(solution)/shard_map/ppermute | solution.py:273
  7.7 0.0 copy-start.2
  7.7 1.2 %copy-done.2 = bf16[2048,256]{1,0:T(8,128)(2,1)S(1)} copy-done((bf16[2048,256]{1,0:T(8,128)(2,1)S(1)}, bf16[2048,256]{1,0:T(8,128)(2,1)}, u32[]{:S(2)}) %copy-start.2) | copy-done | bytes 1048600
  8.9 1.0 %copy-done.3 = bf16[256,1024]{1,0:T(8,128)(2,1)S(1)} copy-done((bf16[256,1024]{1,0:T(8,128)(2,1)S(1)}, bf16[256,1024]{1,0:T(8,128)(2,1)}, u32[]{:S(2)}) %copy-start.3) | copy-done | bytes 524312
  10.0 0.8 %places.1 = (bf16[512,1024]{1,0:T(8,128)(2,1)S(1)}, bf16[2048,256]{1,0:T(8,128)(2,1)S(1)}, bf16[256,1024]{1,0:T(8,128)(2,1)S(1)}) custom-call(s32[1,512]{1,0:T(1,128)S(1)} %bitcast_or_fusion.packed_ref, bf16[2048,256]{1,0:T(8,128)(2,1)S(1)} %copy-done.2, bf16[256,1024]{1,0:T(8,128)(2,1)S(1)} %copy-done.3), custom_call_target="tpu_custom_call" | custom-call | flops 268435456 | bytes 25165824 | tf_op jit(solution)/shard_map/places/pallas_call | solution.py:291
  10.8 0.0 collective-permute-done.refs_0_
  10.8 0.7 %lookup.1 = (bf16[128,256]{1,0:T(8,128)(2,1)S(1)}, bf16[128,256]{1,0:T(8,128)(2,1)S(1)}) custom-call(bf16[2048,256]{1,0:T(8,128)(2,1)S(1)} %get-tuple-element.17.table_ref, s32[1,128]{1,0:T(1,128)S(1)} %collective-permute-done.refs_0_, s32[1,128]{1,0:T(1,128)S(1)} %collective-permute-done.1.refs_1_), custom_call_target="tpu_custom_call" | custom-call | tf_op jit(solution)/shard_map/lookup/pallas_call | solution.py:300
  11.5 2.6 %collective-permute-start.2 = (bf16[128,256]{1,0:T(8,128)(2,1)S(1)}, bf16[128,256]{1,0:T(8,128)(2,1)S(1)}, u32[]{:S(2)}, u32[]{:S(2)}) collective-permute-start(bf16[128,256]{1,0:T(8,128)(2,1)S(1)} %get-tuple-element.20), channel_id=1, source_target_pairs={{0,28},{1,25},{2,22},{3,19},{4,24},{5,29},{6,18},{7,23},{8,20},{9,... | collective-permute-start | bytes 196616 | tf_op jit(solution)/shard_map/ppermute | solution.py:273
  14.1 0.7 %collective-permute-start.3 = (bf16[128,256]{1,0:T(8,128)(2,1)S(1)}, bf16[128,256]{1,0:T(8,128)(2,1)S(1)}, u32[]{:S(2)}, u32[]{:S(2)}) collective-permute-start(bf16[128,256]{1,0:T(8,128)(2,1)S(1)} %get-tuple-element.21), channel_id=1, source_target_pairs={{0,0},{1,5},{2,10},{3,15},{4,4},{5,1},{6,14},{7,11},{8,8},{9,13},{... | collective-permute-start | bytes 196616 | tf_op jit(solution)/shard_map/ppermute | solution.py:273
  14.7 3.8 %collective-permute-done.2 = bf16[128,256]{1,0:T(8,128)(2,1)S(1)} collective-permute-done((bf16[128,256]{1,0:T(8,128)(2,1)S(1)}, bf16[128,256]{1,0:T(8,128)(2,1)S(1)}, u32[]{:S(2)}, u32[]{:S(2)}) %collective-permute-start.2) | collective-permute-done | bytes 65568 | tf_op jit(solution)/shard_map/ppermute | solution.py:273
  18.6 3.1 %collective-permute-start.4 = (bf16[256,256]{1,0:T(8,128)(2,1)S(1)}, bf16[256,256]{1,0:T(8,128)(2,1)S(1)}, u32[]{:S(2)}, u32[]{:S(2)}) collective-permute-start(bf16[256,256]{1,0:T(8,128)(2,1)S(1)} %constant_dynamic-update-slice_fusion.refs_0_), channel_id=1, source_target_pairs={{0,2},{1,3},{2,0},{3,1},{4,6},{5,7},{6,4},{7,5},{8,10},{9,11},{10,... | collective-permute-start | bytes 393224 | tf_op jit(solution)/shard_map/ppermute | solution.py:273
  21.6 2.9 %collective-permute-done.4.refs_1_ = bf16[256,256]{1,0:T(8,128)(2,1)S(1)} collective-permute-done((bf16[256,256]{1,0:T(8,128)(2,1)S(1)}, bf16[256,256]{1,0:T(8,128)(2,1)S(1)}, u32[]{:S(2)}, u32[]{:S(2)}) %collective-permute-start.4) | collective-permute-done | bytes 131104 | tf_op jit(solution)/shard_map/ppermute | solution.py:273
  25.2 0.7 %collective-permute-done.6.refs_3_ = bf16[256,256]{1,0:T(8,128)(2,1)S(1)} collective-permute-done((bf16[256,256]{1,0:T(8,128)(2,1)S(1)}, bf16[256,256]{1,0:T(8,128)(2,1)S(1)}, u32[]{:S(2)}, u32[]{:S(2)}) %collective-permute-start.6) | collective-permute-done | bytes 131104 | tf_op jit(solution)/shard_map/ppermute | solution.py:273
  25.9 22.7 %attend.1 = (bf16[128,1024]{1,0:T(8,128)(2,1)S(1)}, bf16[128,1024]{1,0:T(8,128)(2,1)S(1)}, f32[8,256,128]{2,1,0:T(8,128)S(1)}, bf16[8,256,128]{2,1,0:T(8,128)(2,1)S(1)}) custom-call(s32[1]{0:T(128)S(6)} %copy.11.length_ref, bf16[512,1024]{1,0:T(8,128)(2,1)S(1)} %get-tuple-element.16.places_ref, ...), custom_call_target="tpu_custom_call" | custom-call | tf_op jit(solution)/shard_map/attend/pallas_call | solution.py:316
  48.7 0.1 collective-permute-start.7
  48.7 1.9 %collective-permute-done.7.refs_1_ = bf16[8,256,128]{2,1,0:T(8,128)(2,1)S(1)} collective-permute-done((bf16[8,256,128]{2,1,0:T(8,128)(2,1)S(1)}, bf16[8,256,128]{2,1,0:T(8,128)(2,1)S(1)}, u32[]{:S(2)}, u32[]{:S(2)}) %collective-permute-start.7) | collective-permute-done | bytes 524320 | tf_op jit(solution)/shard_map/ppermute | solution.py:273
  50.6 0.1 add_convert_fusion
  50.7 0.1 collective-permute-start.8
  50.8 0.5 gate.1.refs_3_
  51.3 7.8 %collective-permute-done.8.refs_2_ = bf16[8,128,128]{2,1,0:T(8,128)(2,1)S(1)} collective-permute-done((bf16[8,128,128]{2,1,0:T(8,128)(2,1)S(1)}, bf16[8,128,128]{2,1,0:T(8,128)(2,1)S(1)}, u32[]{:S(2)}, u32[]{:S(2)}) %collective-permute-start.8) | collective-permute-done | bytes 262176 | tf_op jit(solution)/shard_map/ppermute | solution.py:273
  59.1 1.4 %finish.1 = bf16[128,1024]{1,0:T(8,128)(2,1)} custom-call(f32[8,256,128]{2,1,0:T(8,128)S(1)} %get-tuple-element.23.refs_0_, bf16[8,256,128]{2,1,0:T(8,128)(2,1)S(1)} %collective-permute-done.7.refs_1_, bf16[8,128,128]{2,1,0:T(8,128)(2,1)S(1)} %collective-permute-done.8.refs_2_, bf16[128,1024]{1,0:T(8,128)(2,1)S(1)} %gate.1.refs_3_, ...), custom_call_target="tpu_custom_call" | custom-call | tf_op jit(solution)/shard_map/finish/pallas_call | solution.py:357
  (12 shorter events, 0.0 us)
Async XLA Ops:
  1.1 9.7 %collective-permute-start = (s32[1,128]{1,0:T(1,128)S(1)}, s32[1,128]{1,0:T(1,128)S(1)}, u32[]{:S(2)}, u32[]{:S(2)}) collective-permute-start(s32[1,128]{1,0:T(1,128)S(1)} %get-tuple-element.18), channel_id=1, source_target_pairs={{0,28},{1,25},{2,22},{3,19},{4,24},{5,29},{6,18},{7,23},{8,20},{9,... | collective-permute-start | bytes 1544 | tf_op jit(solution)/shard_map/ppermute | solution.py:273
  7.1 3.7 %collective-permute-start.1 = (s32[1,128]{1,0:T(1,128)S(1)}, s32[1,128]{1,0:T(1,128)S(1)}, u32[]{:S(2)}, u32[]{:S(2)}) collective-permute-start(s32[1,128]{1,0:T(1,128)S(1)} %get-tuple-element.19), channel_id=1, source_target_pairs={{0,0},{1,5},{2,10},{3,15},{4,4},{5,1},{6,14},{7,11},{8,8},{9,13},{... | collective-permute-start | bytes 1544 | tf_op jit(solution)/shard_map/ppermute | solution.py:273
  7.7 1.2 %copy-start.2 = (bf16[2048,256]{1,0:T(8,128)(2,1)S(1)}, bf16[2048,256]{1,0:T(8,128)(2,1)}, u32[]{:S(2)}) copy-start(bf16[2048,256]{1,0:T(8,128)(2,1)} %table_ref.1) | copy-start | bytes 3145732
  8.9 1.0 %copy-start.3 = (bf16[256,1024]{1,0:T(8,128)(2,1)S(1)}, bf16[256,1024]{1,0:T(8,128)(2,1)}, u32[]{:S(2)}) copy-start(bf16[256,1024]{1,0:T(8,128)(2,1)} %w_in_ref.1) | copy-start | bytes 1572868
  11.5 7.1 %collective-permute-start.2 = (bf16[128,256]{1,0:T(8,128)(2,1)S(1)}, bf16[128,256]{1,0:T(8,128)(2,1)S(1)}, u32[]{:S(2)}, u32[]{:S(2)}) collective-permute-start(bf16[128,256]{1,0:T(8,128)(2,1)S(1)} %get-tuple-element.20), channel_id=1, source_target_pairs={{0,28},{1,25},{2,22},{3,19},{4,24},{5,29},{6,18},{7,23},{8,20},{9,... | collective-permute-start | bytes 196616 | tf_op jit(solution)/shard_map/ppermute | solution.py:273
  14.1 4.5 %collective-permute-start.3 = (bf16[128,256]{1,0:T(8,128)(2,1)S(1)}, bf16[128,256]{1,0:T(8,128)(2,1)S(1)}, u32[]{:S(2)}, u32[]{:S(2)}) collective-permute-start(bf16[128,256]{1,0:T(8,128)(2,1)S(1)} %get-tuple-element.21), channel_id=1, source_target_pairs={{0,0},{1,5},{2,10},{3,15},{4,4},{5,1},{6,14},{7,11},{8,8},{9,13},{... | collective-permute-start | bytes 196616 | tf_op jit(solution)/shard_map/ppermute | solution.py:273
  18.6 6.0 %collective-permute-start.4 = (bf16[256,256]{1,0:T(8,128)(2,1)S(1)}, bf16[256,256]{1,0:T(8,128)(2,1)S(1)}, u32[]{:S(2)}, u32[]{:S(2)}) collective-permute-start(bf16[256,256]{1,0:T(8,128)(2,1)S(1)} %constant_dynamic-update-slice_fusion.refs_0_), channel_id=1, source_target_pairs={{0,2},{1,3},{2,0},{3,1},{4,6},{5,7},{6,4},{7,5},{8,10},{9,11},{10,... | collective-permute-start | bytes 393224 | tf_op jit(solution)/shard_map/ppermute | solution.py:273
  21.6 3.6 %collective-permute-start.5 = (bf16[256,256]{1,0:T(8,128)(2,1)S(1)}, bf16[256,256]{1,0:T(8,128)(2,1)S(1)}, u32[]{:S(2)}, u32[]{:S(2)}) collective-permute-start(bf16[256,256]{1,0:T(8,128)(2,1)S(1)} %constant_dynamic-update-slice_fusion.refs_0_), channel_id=1, source_target_pairs={{0,1},{1,0},{2,3},{3,2},{4,5},{5,4},{6,7},{7,6},{8,9},{9,8},{10,11... | collective-permute-start | bytes 393224 | tf_op jit(solution)/shard_map/ppermute | solution.py:273
  24.6 1.3 %collective-permute-start.6 = (bf16[256,256]{1,0:T(8,128)(2,1)S(1)}, bf16[256,256]{1,0:T(8,128)(2,1)S(1)}, u32[]{:S(2)}, u32[]{:S(2)}) collective-permute-start(bf16[256,256]{1,0:T(8,128)(2,1)S(1)} %collective-permute-done.4.refs_1_), channel_id=1, source_target_pairs={{0,1},{1,0},{2,3},{3,2},{4,5},{5,4},{6,7},{7,6},{8,9},{9,8},{10,11... | collective-permute-start | bytes 393224 | tf_op jit(solution)/shard_map/ppermute | solution.py:273
  25.9 24.8 %copy-start = (bf16[1024,2048]{1,0:T(8,128)(2,1)S(1)}, bf16[1024,2048]{1,0:T(8,128)(2,1)}, u32[]{:S(2)}) copy-start(bf16[1024,2048]{1,0:T(8,128)(2,1)} %w_uq_ref.1) | copy-start | bytes 12582916
  25.9 33.2 %copy-start.1 = (bf16[1024,1024]{1,0:T(8,128)(2,1)S(1)}, bf16[1024,1024]{1,0:T(8,128)(2,1)}, u32[]{:S(2)}) copy-start(bf16[1024,1024]{1,0:T(8,128)(2,1)} %refs_5_.3) | copy-start | bytes 6291460
  48.7 2.0 %collective-permute-start.7 = (bf16[8,256,128]{2,1,0:T(8,128)(2,1)S(1)}, bf16[8,256,128]{2,1,0:T(8,128)(2,1)S(1)}, u32[]{:S(2)}, u32[]{:S(2)}) collective-permute-start(bf16[8,256,128]{2,1,0:T(8,128)(2,1)S(1)} %get-tuple-element.24), channel_id=1, source_target_pairs={{0,1},{1,0},{2,3},{3,2},{4,5},{5,4},{6,7},{7,6},{8,9},{9,8},{10,11... | collective-permute-start | bytes 1572872 | tf_op jit(solution)/shard_map/ppermute | solution.py:273
  50.7 8.4 %collective-permute-start.8 = (bf16[8,128,128]{2,1,0:T(8,128)(2,1)S(1)}, bf16[8,128,128]{2,1,0:T(8,128)(2,1)S(1)}, u32[]{:S(2)}, u32[]{:S(2)}) collective-permute-start(bf16[8,128,128]{2,1,0:T(8,128)(2,1)S(1)} %add_convert_fusion), channel_id=1, source_target_pairs={{0,2},{1,3},{2,0},{3,1},{4,6},{5,7},{6,4},{7,5},{8,10},{9,11},{10,... | collective-permute-start | bytes 786440 | tf_op jit(solution)/shard_map/ppermute | solution.py:273

commit v4 on v3

--- a/solution.py
+++ b/solution.py
@@ -80,9 +80,13 @@
         list_refs[turn][...] = packed.astype(jnp.int32)
 
 
-def places_kernel(per, cap, turns, packed_ref, table_ref, w_in_ref, places_ref, *held):
-    held[0][...] = table_ref[...]
-    held[1][...] = w_in_ref[...]
+def hold_kernel(table_ref, held_ref):
+    held_ref[...] = table_ref[...]
+
+
+def places_kernel(per, cap, turns, packed_ref, rows_ref, w_in_ref, places_ref, held_ref):
+    del rows_ref
+    held_ref[...] = w_in_ref[...]
     peers = lax.axis_size("ctx")
     me = lax.axis_index("ctx")
     codes, rank = ranks(packed_ref[...], per)
@@ -116,6 +120,7 @@
 
 
 def lookup_kernel(turns, table_ref, *refs):
+    refs[-1][...] = jnp.zeros_like(refs[-1])
     for list_ref, rows_ref in zip(refs[:turns], refs[turns:]):
         length = list_ref.shape[1]
         same = (iota((length, length), 0) == iota((length, length), 1)).astype(F32).astype(BF16)
@@ -128,8 +133,8 @@
 def attend_kernel(per, buffers, length_ref, places_ref, *refs):
     received, refs = refs[:buffers], refs[buffers:]
     w_in_ref, w_uq_hbm, keys_hbm, values_hbm = refs[:4]
-    features_ref, normed_ref, keep_ref, send_ref = refs[4:8]
-    queries_ref, keys_ref, values_ref, w_query_ref, sems, weight_sem = refs[8:]
+    features_ref, normed_ref, keep_ref, near_ref, far_ref = refs[4:9]
+    queries_ref, keys_ref, values_ref, w_query_ref, sems, weight_sem = refs[9:]
     heads, events, head_dim = keys_ref.shape
     width = heads * head_dim
     kept = keep_ref.shape[1]
@@ -204,7 +209,8 @@
 
     def store(head, total):
         keep_ref[head] = total[:kept]
-        send_ref[head] = total[kept:].astype(BF16)
+        near_ref[head] = total[kept : kept + per].astype(BF16)
+        far_ref[head] = total[kept + per :].astype(BF16)
 
     zero = jnp.zeros((queries_ref.shape[1], head_dim), F32)
 
@@ -212,10 +218,11 @@
     def _():
         @pl.loop(0, heads // 4)
         def _(head):
-            for one in [4 * head + extra for extra in range(4)]:
-                for copy in copies(one):
-                    copy.wait()
-            for one in [4 * head + extra for extra in range(4)]:
+            for extra in range(4):
+                one = 4 * head + extra
+                if extra % 2 == 0:
+                    for copy in copies(one) + copies(one + 1):
+                        copy.wait()
                 total = zero
                 for first in range(0, events, group):
                     total = add_group(one, first, total, first + group >= events)
@@ -240,12 +247,12 @@
 
 
 def finish_kernel(others, *refs):
-    keep_ref, sibling_ref = refs[:2]
-    gate_ref, features_ref, w_out_ref, out_ref = refs[2 + others :]
+    keep_ref = refs[0]
+    gate_ref, features_ref, w_out_ref, out_ref = refs[1 + others :]
     parts = []
     for head in range(keep_ref.shape[0]):
-        part = keep_ref[head] + sibling_ref[head].astype(F32)
-        for other in refs[2 : 2 + others]:
+        part = keep_ref[head]
+        for other in refs[1 : 1 + others]:
             part = part + other[head].astype(F32)
         parts.append(part)
     attended = jnp.concatenate(parts, axis=1)
@@ -288,24 +295,35 @@
         name="requests",
     )(packed)
     asked = [swap_owner(lists[turn], turn) for turn in reversed(range(turns))][::-1]
-    places, table, w_in = pl.pallas_call(
+    table = pl.pallas_call(
+        hold_kernel,
+        in_specs=[VMEM],
+        out_specs=VMEM,
+        out_shape=shape(item_table.shape, BF16),
+        compiler_params=params(16),
+        cost_estimate=pl.CostEstimate(flops=1 << 20, bytes_accessed=24 << 20, transcendentals=0),
+        name="hold",
+    )(item_table)
+    looked = pl.pallas_call(
+        functools.partial(lookup_kernel, turns),
+        in_specs=[VMEM] * (1 + turns),
+        out_specs=[VMEM] * (turns + 1),
+        out_shape=[shape((length, item_table.shape[1]), BF16)] * turns
+        + [shape((8, 128), BF16)],
+        compiler_params=params(16),
+        name="lookup",
+    )(table, *asked)
+    places, w_in = pl.pallas_call(
         functools.partial(places_kernel, per, cap, turns),
         in_specs=[VMEM] * 3,
-        out_specs=[VMEM] * 3,
-        out_shape=[shape((count, users * length), BF16), shape(item_table.shape, BF16), shape(w_in.shape, BF16)],
+        out_specs=[VMEM] * 2,
+        out_shape=[shape((count, users * length), BF16), shape(w_in.shape, BF16)],
         compiler_params=params(16),
         cost_estimate=pl.CostEstimate(flops=1 << 28, bytes_accessed=24 << 20, transcendentals=0),
         name="places",
-    )(packed, item_table, w_in)
-    rows = pl.pallas_call(
-        functools.partial(lookup_kernel, turns),
-        in_specs=[VMEM] * (1 + turns),
-        out_specs=[VMEM] * turns,
-        out_shape=[shape((length, item_table.shape[1]), BF16)] * turns,
-        compiler_params=params(16),
-        name="lookup",
-    )(table, *asked)
-    rows = [swap_owner(rows[turn], turn) for turn in reversed(range(turns))][::-1]
+    )(packed, looked[-1], w_in)
+    rows = [swap_owner(looked[turn], turn) for turn in reversed(range(turns))][::-1]
+    *rows, places, w_in = lax.optimization_barrier((*rows, places, w_in))
     buffers = [jnp.concatenate(rows, axis=0)]
     for step in exchange_steps(peers):
         buffers = buffers + [swap_peer(one, step) for one in buffers]
@@ -313,15 +331,16 @@
     events = keys.shape[0]
     head_dim = width // HEADS
     half = count // 2
-    features, normed, keep, send = pl.pallas_call(
+    features, normed, keep, near, far = pl.pallas_call(
         functools.partial(attend_kernel, per, len(buffers)),
         in_specs=[SMEM] + [VMEM] * (1 + len(buffers)) + [VMEM] + [HBM] * 3,
-        out_specs=[VMEM] * 4,
+        out_specs=[VMEM] * 5,
         out_shape=[
             shape((per, width), BF16),
             shape((per, width), BF16),
             shape((HEADS, half, head_dim), F32),
-            shape((HEADS, half, head_dim), BF16),
+            shape((HEADS, per, head_dim), BF16),
+            shape((HEADS, half - per, head_dim), BF16),
         ],
         scratch_shapes=[
             pltpu.VMEM((HEADS, count, head_dim), BF16),
@@ -347,24 +366,27 @@
         cost_estimate=pl.CostEstimate(flops=1 << 28, bytes_accessed=3 << 20, transcendentals=0),
         name="gate",
     )(normed, w_uq)
-    sibling = swap_peer(send, 1)
-    others = []
+    sibling = swap_peer(far, 1)
+    sums = []
     for index in range(1, peers // 2):
-        piece = slice(index * per, (index + 1) * per)
-        summed = (keep[:, piece] + sibling[:, piece].astype(F32)).astype(BF16)
-        others.append(swap_peer(summed, 2 * index))
+        piece = slice((index - 1) * per, index * per)
+        kept = keep[:, index * per : (index + 1) * per]
+        sums.append((kept + sibling[:, piece].astype(F32)).astype(BF16))
+    near, *sums = lax.optimization_barrier((near, *sums))
+    others = [swap_peer(one, 2 * index) for index, one in enumerate(sums, 1)]
+    others.append(swap_peer(near, 1))
     block = pl.BlockSpec((HEADS, per, head_dim), lambda i: (0, 0, 0))
     ranked = pl.pallas_call(
         functools.partial(finish_kernel, len(others)),
         grid=(1,),
-        in_specs=[block] * (2 + len(others))
+        in_specs=[block] * (1 + len(others))
         + [pl.BlockSpec((per, width), lambda i: (0, 0))] * 2
         + [pl.BlockSpec((width, width), lambda i: (0, 0))],
         out_specs=pl.BlockSpec((per, width), lambda i: (0, 0)),
         out_shape=shape((per, width), BF16),
         compiler_params=params(24),
         name="finish",
-    )(keep, sibling, *others, gate, features, w_out)
+    )(keep, *others, gate, features, w_out)
     return ranked[None]
 
 

time: 61.2 us -> 58.7 us (0.959)
  the two profiles are of different devices: /device:TPU:0 before, /device:TPU:12 now
where the time goes in v4:
time: 58.7 us; the launch traced here: 57.7 us
  Pallas kernels  26.2 us (45%)
  waiting for transfers between devices  18.6 us (32%)
  starting transfers between devices  9.08 us (15%)
  local copies, waits for them, and re-layouts  2.28 us (4%)
  between operations  0.79 us (1%)
  other arithmetic  0.76 us (1%)
    pallas_call x1, Pallas kernels, shards(): pl.pallas_call(functools.partial(attend_kernel, per, len(buffers)), in_sp...  22.5 us
    ppermute x10, waiting for transfers between devices, permute(): return lax.ppermute(values, ('req', 'ctx'), pairs)  18.6 us
    ppermute x10, starting transfers between devices, permute(): return lax.ppermute(values, ('req', 'ctx'), pairs)  9.08 us
    unnamed x9, local copies, waits for them, and re-layouts  2.27 us
    pallas_call x1, Pallas kernels, shards(): pl.pallas_call(functools.partial(finish_kernel, len(others)), grid=(1,),...  1.35 us
  transfers between devices with their start and end apart: 10, of which 6 were waited for; matrix products, arithmetic and copies ran while one was open for 0% of the time, Pallas kernels for 2%

profile of v4, /device:TPU:12, one launch (start us, length us, event | category | flops | bytes accessed | tf_op | source)
XLA Modules:
  0.0 57.7 jit_solution(11133677157313449471)
XLA Ops:
  0.0 0.7 %bitcast_or_fusion.packed_ref = s32[1,512]{1,0:T(1,128)S(1)} fusion(s32[1,512]{1,0:T(1,128)} %param.11, s32[1,512,1]{1,2,0:T(1,128)} %param.10), kind=kLoop, calls=%fused_computation.3 | loop fusion | flops 1024 | bytes 6144 | tf_op jit(solution)/shard_map/or | solution.py:288
  0.7 0.4 requests.1
  1.1 3.5 %collective-permute-start = (s32[1,128]{1,0:T(1,128)S(1)}, s32[1,128]{1,0:T(1,128)S(1)}, u32[]{:S(2)}, u32[]{:S(2)}) collective-permute-start(s32[1,128]{1,0:T(1,128)S(1)} %get-tuple-element.23), channel_id=1, source_target_pairs={{0,28},{1,25},{2,22},{3,19},{4,24},{5,29},{6,18},{7,23},{8,20},{9,... | collective-permute-start | bytes 1544 | tf_op jit(solution)/shard_map/ppermute | solution.py:280
  4.6 2.3 %collective-permute-start.1 = (s32[1,128]{1,0:T(1,128)S(1)}, s32[1,128]{1,0:T(1,128)S(1)}, u32[]{:S(2)}, u32[]{:S(2)}) collective-permute-start(s32[1,128]{1,0:T(1,128)S(1)} %get-tuple-element.24), channel_id=1, source_target_pairs={{0,0},{1,5},{2,10},{3,15},{4,4},{5,1},{6,14},{7,11},{8,8},{9,13},{... | collective-permute-start | bytes 1544 | tf_op jit(solution)/shard_map/ppermute | solution.py:280
  7.0 1.2 %copy-done.2 = bf16[2048,256]{1,0:T(8,128)(2,1)S(1)} copy-done((bf16[2048,256]{1,0:T(8,128)(2,1)S(1)}, bf16[2048,256]{1,0:T(8,128)(2,1)}, u32[]{:S(2)}) %copy-start.2) | copy-done | bytes 1048600
  8.3 1.8 %collective-permute-done.1.refs_1_ = s32[1,128]{1,0:T(1,128)S(1)} collective-permute-done((s32[1,128]{1,0:T(1,128)S(1)}, s32[1,128]{1,0:T(1,128)S(1)}, u32[]{:S(2)}, u32[]{:S(2)}) %collective-permute-start.1) | collective-permute-done | bytes 544 | tf_op jit(solution)/shard_map/ppermute | solution.py:280
  10.0 0.7 %lookup.1 = (bf16[128,256]{1,0:T(8,128)(2,1)S(1)}, bf16[128,256]{1,0:T(8,128)(2,1)S(1)}, bf16[8,128]{1,0:T(8,128)(2,1)S(1)}) custom-call(bf16[2048,256]{1,0:T(8,128)(2,1)S(1)} %hold.1.table_ref, s32[1,128]{1,0:T(1,128)S(1)} %collective-permute-done.refs_0_, s32[1,128]{1,0:T(1,128)S(1)} %collective-permute-done.1.refs_1_), custom_call_target="tpu_custom_call" | custom-call | tf_op jit(solution)/shard_map/lookup/pallas_call | solution.py:307
  10.7 0.4 collective-permute-start.2
  11.1 2.3 %collective-permute-start.3 = (bf16[128,256]{1,0:T(8,128)(2,1)S(1)}, bf16[128,256]{1,0:T(8,128)(2,1)S(1)}, u32[]{:S(2)}, u32[]{:S(2)}) collective-permute-start(bf16[128,256]{1,0:T(8,128)(2,1)S(1)} %get-tuple-element.26), channel_id=1, source_target_pairs={{0,0},{1,5},{2,10},{3,15},{4,4},{5,1},{6,14},{7,11},{8,8},{9,13},{... | collective-permute-start | bytes 196616 | tf_op jit(solution)/shard_map/ppermute | solution.py:280
  13.4 1.0 %copy-done.3 = bf16[256,1024]{1,0:T(8,128)(2,1)S(1)} copy-done((bf16[256,1024]{1,0:T(8,128)(2,1)S(1)}, bf16[256,1024]{1,0:T(8,128)(2,1)}, u32[]{:S(2)}) %copy-start.3) | copy-done | bytes 524312
  14.5 0.7 %places.1 = (bf16[512,1024]{1,0:T(8,128)(2,1)S(1)}, bf16[256,1024]{1,0:T(8,128)(2,1)S(1)}) custom-call(s32[1,512]{1,0:T(1,128)S(1)} %bitcast_or_fusion.packed_ref, bf16[8,128]{1,0:T(8,128)(2,1)S(1)} %get-tuple-element.27.rows_ref, bf16[256,1024]{1,0:T(8,128)(2,1)S(1)} %copy-done.3), custom_call_target="tpu_custom_call" | custom-call | flops 268435456 | bytes 25165824 | tf_op jit(solution)/shard_map/places/pallas_call | solution.py:316
  15.2 2.1 %collective-permute-done.2 = bf16[128,256]{1,0:T(8,128)(2,1)S(1)} collective-permute-done((bf16[128,256]{1,0:T(8,128)(2,1)S(1)}, bf16[128,256]{1,0:T(8,128)(2,1)S(1)}, u32[]{:S(2)}, u32[]{:S(2)}) %collective-permute-start.2) | collective-permute-done | bytes 65568 | tf_op jit(solution)/shard_map/ppermute | solution.py:280
  17.3 0.1 collective-permute-start.4
  17.4 0.1 collective-permute-start.5
  17.5 4.9 %collective-permute-done.4.refs_1_ = bf16[256,256]{1,0:T(8,128)(2,1)S(1)} collective-permute-done((bf16[256,256]{1,0:T(8,128)(2,1)S(1)}, bf16[256,256]{1,0:T(8,128)(2,1)S(1)}, u32[]{:S(2)}, u32[]{:S(2)}) %collective-permute-start.4) | collective-permute-done | bytes 131104 | tf_op jit(solution)/shard_map/ppermute | solution.py:280
  23.0 0.7 %collective-permute-done.6.refs_3_ = bf16[256,256]{1,0:T(8,128)(2,1)S(1)} collective-permute-done((bf16[256,256]{1,0:T(8,128)(2,1)S(1)}, bf16[256,256]{1,0:T(8,128)(2,1)S(1)}, u32[]{:S(2)}, u32[]{:S(2)}) %collective-permute-start.6) | collective-permute-done | bytes 131104 | tf_op jit(solution)/shard_map/ppermute | solution.py:280
  23.7 22.5 %attend.1 = (bf16[128,1024]{1,0:T(8,128)(2,1)S(1)}, bf16[128,1024]{1,0:T(8,128)(2,1)S(1)}, f32[8,256,128]{2,1,0:T(8,128)S(1)}, bf16[8,128,128]{2,1,0:T(8,128)(2,1)S(1)}, bf16[8,128,128]{2,1,0:T(8,128)(2,1)S(1)}) custom-call(s32[1]{0:T(128)S(6)} %copy.11.length_ref, bf16[512,1024]{1,0:T(8,128)(2,1)S(1)} %get-tuple-element.30.places_ref, ...), custom_call_target="tpu_custom_call" | custom-call | tf_op jit(solution)/shard_map/attend/pallas_call | solution.py:334
  46.2 0.1 collective-permute-start.7
  46.3 1.5 %collective-permute-done.7 = bf16[8,128,128]{2,1,0:T(8,128)(2,1)S(1)} collective-permute-done((bf16[8,128,128]{2,1,0:T(8,128)(2,1)S(1)}, bf16[8,128,128]{2,1,0:T(8,128)(2,1)S(1)}, u32[]{:S(2)}, u32[]{:S(2)}) %collective-permute-start.7) | collective-permute-done | bytes 262176 | tf_op jit(solution)/shard_map/ppermute | solution.py:280
  47.9 0.1 collective-permute-start.8
  48.0 0.2 collective-permute-start.9
  48.2 0.5 gate.1.refs_3_
  48.7 7.6 %collective-permute-done.8.refs_1_ = bf16[8,128,128]{2,1,0:T(8,128)(2,1)S(1)} collective-permute-done((bf16[8,128,128]{2,1,0:T(8,128)(2,1)S(1)}, bf16[8,128,128]{2,1,0:T(8,128)(2,1)S(1)}, u32[]{:S(2)}, u32[]{:S(2)}) %collective-permute-start.8) | collective-permute-done | bytes 262176 | tf_op jit(solution)/shard_map/ppermute | solution.py:280
  56.3 1.4 %finish.1 = bf16[128,1024]{1,0:T(8,128)(2,1)} custom-call(f32[8,256,128]{2,1,0:T(8,128)S(1)} %get-tuple-element.34.refs_0_, bf16[8,128,128]{2,1,0:T(8,128)(2,1)S(1)} %collective-permute-done.8.refs_1_, bf16[8,128,128]{2,1,0:T(8,128)(2,1)S(1)} %collective-permute-done.9.refs_2_, bf16[128,1024]{1,0:T(8,128)(2,1)S(1)} %gate.1.refs_3_, ...), custom_call_target="tpu_custom_call" | custom-call | tf_op jit(solution)/shard_map/finish/pallas_call | solution.py:379
  (15 shorter events, 0.2 us)
Async XLA Ops:
  1.1 7.2 %collective-permute-start = (s32[1,128]{1,0:T(1,128)S(1)}, s32[1,128]{1,0:T(1,128)S(1)}, u32[]{:S(2)}, u32[]{:S(2)}) collective-permute-start(s32[1,128]{1,0:T(1,128)S(1)} %get-tuple-element.23), channel_id=1, source_target_pairs={{0,28},{1,25},{2,22},{3,19},{4,24},{5,29},{6,18},{7,23},{8,20},{9,... | collective-permute-start | bytes 1544 | tf_op jit(solution)/shard_map/ppermute | solution.py:280
  4.6 5.4 %collective-permute-start.1 = (s32[1,128]{1,0:T(1,128)S(1)}, s32[1,128]{1,0:T(1,128)S(1)}, u32[]{:S(2)}, u32[]{:S(2)}) collective-permute-start(s32[1,128]{1,0:T(1,128)S(1)} %get-tuple-element.24), channel_id=1, source_target_pairs={{0,0},{1,5},{2,10},{3,15},{4,4},{5,1},{6,14},{7,11},{8,8},{9,13},{... | collective-permute-start | bytes 1544 | tf_op jit(solution)/shard_map/ppermute | solution.py:280
  6.9 1.2 %copy-start.2 = (bf16[2048,256]{1,0:T(8,128)(2,1)S(1)}, bf16[2048,256]{1,0:T(8,128)(2,1)}, u32[]{:S(2)}) copy-start(bf16[2048,256]{1,0:T(8,128)(2,1)} %table_ref.1) | copy-start | bytes 3145732
  10.7 6.6 %collective-permute-start.2 = (bf16[128,256]{1,0:T(8,128)(2,1)S(1)}, bf16[128,256]{1,0:T(8,128)(2,1)S(1)}, u32[]{:S(2)}, u32[]{:S(2)}) collective-permute-start(bf16[128,256]{1,0:T(8,128)(2,1)S(1)} %get-tuple-element.25), channel_id=1, source_target_pairs={{0,28},{1,25},{2,22},{3,19},{4,24},{5,29},{6,18},{7,23},{8,20},{9,... | collective-permute-start | bytes 196616 | tf_op jit(solution)/shard_map/ppermute | solution.py:280
  11.1 6.2 %collective-permute-start.3 = (bf16[128,256]{1,0:T(8,128)(2,1)S(1)}, bf16[128,256]{1,0:T(8,128)(2,1)S(1)}, u32[]{:S(2)}, u32[]{:S(2)}) collective-permute-start(bf16[128,256]{1,0:T(8,128)(2,1)S(1)} %get-tuple-element.26), channel_id=1, source_target_pairs={{0,0},{1,5},{2,10},{3,15},{4,4},{5,1},{6,14},{7,11},{8,8},{9,13},{... | collective-permute-start | bytes 196616 | tf_op jit(solution)/shard_map/ppermute | solution.py:280
  13.4 1.0 %copy-start.3 = (bf16[256,1024]{1,0:T(8,128)(2,1)S(1)}, bf16[256,1024]{1,0:T(8,128)(2,1)}, u32[]{:S(2)}) copy-start(bf16[256,1024]{1,0:T(8,128)(2,1)} %w_in_ref.1) | copy-start | bytes 1572868
  17.3 5.0 %collective-permute-start.4 = (bf16[256,256]{1,0:T(8,128)(2,1)S(1)}, bf16[256,256]{1,0:T(8,128)(2,1)S(1)}, u32[]{:S(2)}, u32[]{:S(2)}) collective-permute-start(bf16[256,256]{1,0:T(8,128)(2,1)S(1)} %constant_dynamic-update-slice_fusion.refs_0_), channel_id=1, source_target_pairs={{0,2},{1,3},{2,0},{3,1},{4,6},{5,7},{6,4},{7,5},{8,10},{9,11},{10,... | collective-permute-start | bytes 393224 | tf_op jit(solution)/shard_map/ppermute | solution.py:280
  17.4 5.6 %collective-permute-start.5 = (bf16[256,256]{1,0:T(8,128)(2,1)S(1)}, bf16[256,256]{1,0:T(8,128)(2,1)S(1)}, u32[]{:S(2)}, u32[]{:S(2)}) collective-permute-start(bf16[256,256]{1,0:T(8,128)(2,1)S(1)} %constant_dynamic-update-slice_fusion.refs_0_), channel_id=1, source_target_pairs={{0,1},{1,0},{2,3},{3,2},{4,5},{5,4},{6,7},{7,6},{8,9},{9,8},{10,11... | collective-permute-start | bytes 393224 | tf_op jit(solution)/shard_map/ppermute | solution.py:280
  22.3 1.3 %collective-permute-start.6 = (bf16[256,256]{1,0:T(8,128)(2,1)S(1)}, bf16[256,256]{1,0:T(8,128)(2,1)S(1)}, u32[]{:S(2)}, u32[]{:S(2)}) collective-permute-start(bf16[256,256]{1,0:T(8,128)(2,1)S(1)} %collective-permute-done.4.refs_1_), channel_id=1, source_target_pairs={{0,1},{1,0},{2,3},{3,2},{4,5},{5,4},{6,7},{7,6},{8,9},{9,8},{10,11... | collective-permute-start | bytes 393224 | tf_op jit(solution)/shard_map/ppermute | solution.py:280
  23.7 24.5 %copy-start = (bf16[1024,2048]{1,0:T(8,128)(2,1)S(1)}, bf16[1024,2048]{1,0:T(8,128)(2,1)}, u32[]{:S(2)}) copy-start(bf16[1024,2048]{1,0:T(8,128)(2,1)} %w_uq_ref.1) | copy-start | bytes 12582916
  23.7 32.6 %copy-start.1 = (bf16[1024,1024]{1,0:T(8,128)(2,1)S(1)}, bf16[1024,1024]{1,0:T(8,128)(2,1)}, u32[]{:S(2)}) copy-start(bf16[1024,1024]{1,0:T(8,128)(2,1)} %refs_5_.3) | copy-start | bytes 6291460
  46.2 1.6 %collective-permute-start.7 = (bf16[8,128,128]{2,1,0:T(8,128)(2,1)S(1)}, bf16[8,128,128]{2,1,0:T(8,128)(2,1)S(1)}, u32[]{:S(2)}, u32[]{:S(2)}) collective-permute-start(bf16[8,128,128]{2,1,0:T(8,128)(2,1)S(1)} %get-tuple-element.36), channel_id=1, source_target_pairs={{0,1},{1,0},{2,3},{3,2},{4,5},{5,4},{6,7},{7,6},{8,9},{9,8},{10,11... | collective-permute-start | bytes 786440 | tf_op jit(solution)/shard_map/ppermute | solution.py:280
  47.9 8.4 %collective-permute-start.8 = (bf16[8,128,128]{2,1,0:T(8,128)(2,1)S(1)}, bf16[8,128,128]{2,1,0:T(8,128)(2,1)S(1)}, u32[]{:S(2)}, u32[]{:S(2)}) collective-permute-start(bf16[8,128,128]{2,1,0:T(8,128)(2,1)S(1)} %add_convert_fusion), channel_id=1, source_target_pairs={{0,2},{1,3},{2,0},{3,1},{4,6},{5,7},{6,4},{7,5},{8,10},{9,11},{10,... | collective-permute-start | bytes 786440 | tf_op jit(solution)/shard_map/ppermute | solution.py:280
  48.0 8.3 %collective-permute-start.9 = (bf16[8,128,128]{2,1,0:T(8,128)(2,1)S(1)}, bf16[8,128,128]{2,1,0:T(8,128)(2,1)S(1)}, u32[]{:S(2)}, u32[]{:S(2)}) collective-permute-start(bf16[8,128,128]{2,1,0:T(8,128)(2,1)S(1)} %get-tuple-element.38), channel_id=1, source_target_pairs={{0,1},{1,0},{2,3},{3,2},{4,5},{5,4},{6,7},{7,6},{8,9},{9,8},{10,11... | collective-permute-start | bytes 786440 | tf_op jit(solution)/shard_map/ppermute | solution.py:280

commit v5 on v4

--- a/solution.py
+++ b/solution.py
@@ -8,6 +8,7 @@
 from jax.sharding import PartitionSpec as P
 
 HEADS = 8
+CORES = 2
 KEY_BLOCK = 256
 GROUP = 1024
 VMEM = pl.BlockSpec(memory_space=pltpu.VMEM)
@@ -61,8 +62,8 @@
     return codes, rank.astype(jnp.int32)
 
 
-def code_of(peer, turn, peers):
-    return turn * peers + (peer if turn % 2 == 0 else peers - 1 - peer)
+def code_of(core, turn):
+    return turn * CORES + (core if turn % 2 == 0 else CORES - 1 - core)
 
 
 def requests_kernel(per, cap, turns, packed_ref, *list_refs):
@@ -72,7 +73,7 @@
     parts = hi_lo(packed_ref[...] & 65535)
     length = peers * cap
     for turn in range(turns):
-        code = code_of(lax.axis_index("ctx"), turn, peers)
+        code = code_of(lax.axis_index("ctx") % CORES, turn)
         wanted = jnp.where(codes == code, place, -1)
         chosen = (iota((length, codes.shape[1]), 0) == wanted).astype(F32).astype(BF16)
         packed = lax.dot_general(parts, chosen, NT, preferred_element_type=F32)
@@ -80,7 +81,8 @@
         list_refs[turn][...] = packed.astype(jnp.int32)
 
 
-def hold_kernel(table_ref, held_ref):
+def hold_kernel(table_ref, held_ref, done_ref):
+    done_ref[...] = jnp.zeros_like(done_ref)
     held_ref[...] = table_ref[...]
 
 
@@ -92,12 +94,10 @@
     codes, rank = ranks(packed_ref[...], per)
     count = codes.shape[1]
     length = peers * cap
-    turn = codes // peers
-    inner = codes % peers
-    peer = jnp.where(turn % 2 == 0, inner, peers - 1 - inner) ^ me
-    buffer = jnp.zeros_like(peer)
-    for bit, step in enumerate(exchange_steps(peers)):
-        buffer = buffer + jnp.where((peer & step) != 0, 1 << bit, 0)
+    turn = codes // CORES
+    inner = codes % CORES
+    core = jnp.where(turn % 2 == 0, inner, CORES - 1 - inner)
+    buffer = jnp.where(core == me % CORES, 0, 1)
     place = (buffer * turns + turn) * length + (iota(codes.shape, 1) // per) * cap + rank
     row, column = iota((count, count), 0), iota((count, count), 1)
     block = row // per
@@ -111,23 +111,20 @@
     places_ref[...] = (iota((count, total), 1) == found).astype(F32).astype(BF16)
 
 
-def exchange_steps(peers):
-    steps, step = [], peers // 2
-    while step >= 1:
-        steps.append(step)
-        step //= 2
-    return steps
-
-
-def lookup_kernel(turns, table_ref, *refs):
+def lookup_kernel(turns, table_ref, done_ref, *refs):
+    del done_ref
     refs[-1][...] = jnp.zeros_like(refs[-1])
     for list_ref, rows_ref in zip(refs[:turns], refs[turns:]):
         length = list_ref.shape[1]
         same = (iota((length, length), 0) == iota((length, length), 1)).astype(F32).astype(BF16)
         found = lax.dot_general(same, hi_lo(list_ref[...]), NT, preferred_element_type=F32)
-        found = (found[:, 0:1] * 256.0 + found[:, 1:2]).astype(jnp.int32)
-        chosen = (iota((length, table_ref.shape[0]), 1) == found).astype(F32).astype(BF16)
-        rows_ref[...] = dot(chosen, table_ref[...]).astype(BF16)
+        high, low = found[:, 0:1].astype(jnp.int32), found[:, 1:2].astype(jnp.int32)
+        parts = table_ref.shape[0] // 256
+        same_low = iota((length, 256), 1) == low
+        chosen = [
+            jnp.where(same_low & (high == part), 1.0, 0.0).astype(BF16) for part in range(parts)
+        ]
+        rows_ref[...] = dot(jnp.concatenate(chosen, axis=1), table_ref[...]).astype(BF16)
 
 
 def attend_kernel(per, buffers, length_ref, places_ref, *refs):
@@ -266,7 +263,7 @@
     count = cand_owner.shape[1]
     per = count // peers
     cap = max(2, 2 * per // users)
-    turns = users // peers
+    turns = users // CORES
     length = peers * cap
     width = w_out.shape[0]
     shape = jax.ShapeDtypeStruct
@@ -280,7 +277,7 @@
         return lax.ppermute(values, ("req", "ctx"), pairs)
 
     def swap_owner(values, turn):
-        return permute(values, lambda user, peer: (user ^ (users - 1) ^ code_of(peer, turn, peers), peer))
+        return permute(values, lambda user, peer: (user ^ (users - 1) ^ code_of(peer % CORES, turn), peer))
 
     def swap_peer(values, step):
         return permute(values, lambda user, peer: (user, peer ^ step))
@@ -295,24 +292,27 @@
         name="requests",
     )(packed)
     asked = [swap_owner(lists[turn], turn) for turn in reversed(range(turns))][::-1]
-    table = pl.pallas_call(
+    table, table_done = pl.pallas_call(
         hold_kernel,
         in_specs=[VMEM],
-        out_specs=VMEM,
-        out_shape=shape(item_table.shape, BF16),
+        out_specs=[VMEM] * 2,
+        out_shape=[shape(item_table.shape, BF16), shape((8, 128), BF16)],
         compiler_params=params(16),
         cost_estimate=pl.CostEstimate(flops=1 << 20, bytes_accessed=24 << 20, transcendentals=0),
         name="hold",
     )(item_table)
-    looked = pl.pallas_call(
-        functools.partial(lookup_kernel, turns),
-        in_specs=[VMEM] * (1 + turns),
-        out_specs=[VMEM] * (turns + 1),
-        out_shape=[shape((length, item_table.shape[1]), BF16)] * turns
-        + [shape((8, 128), BF16)],
-        compiler_params=params(16),
-        name="lookup",
-    )(table, *asked)
+    looked, looked_done = [], table_done
+    for group in (asked[: turns // 2], asked[turns // 2 :]):
+        *found, looked_done = pl.pallas_call(
+            functools.partial(lookup_kernel, len(group)),
+            in_specs=[VMEM] * (2 + len(group)),
+            out_specs=[VMEM] * (len(group) + 1),
+            out_shape=[shape((length, item_table.shape[1]), BF16)] * len(group)
+            + [shape((8, 128), BF16)],
+            compiler_params=params(16),
+            name="lookup",
+        )(table, looked_done, *group)
+        looked = looked + found
     places, w_in = pl.pallas_call(
         functools.partial(places_kernel, per, cap, turns),
         in_specs=[VMEM] * 3,
@@ -321,12 +321,11 @@
         compiler_params=params(16),
         cost_estimate=pl.CostEstimate(flops=1 << 28, bytes_accessed=24 << 20, transcendentals=0),
         name="places",
-    )(packed, looked[-1], w_in)
+    )(packed, looked_done, w_in)
     rows = [swap_owner(looked[turn], turn) for turn in reversed(range(turns))][::-1]
     *rows, places, w_in = lax.optimization_barrier((*rows, places, w_in))
-    buffers = [jnp.concatenate(rows, axis=0)]
-    for step in exchange_steps(peers):
-        buffers = buffers + [swap_peer(one, step) for one in buffers]
+    fetched = jnp.concatenate(rows, axis=0)
+    buffers = [fetched, swap_peer(fetched, 1)]
     keys, values = k_cache[0], v_cache[0]
     events = keys.shape[0]
     head_dim = width // HEADS

time: 58.7 us -> 58.7 us (level)
  the two profiles are of different devices: /device:TPU:12 before, /device:TPU:0 now
where the time goes in v5:
time: 58.7 us; the launch traced here: 58 us
  Pallas kernels  27.1 us (46%)
  starting transfers between devices  14.4 us (25%)
  waiting for transfers between devices  12.7 us (22%)
  local copies, waits for them, and re-layouts  2.29 us (4%)
  between operations  0.79 us (1%)
  other arithmetic  0.76 us (1%)
    pallas_call x1, Pallas kernels, shards(): pl.pallas_call(functools.partial(attend_kernel, per, len(buffers)), in_sp...  22.5 us
    ppermute x12, starting transfers between devices, permute(): return lax.ppermute(values, ('req', 'ctx'), pairs)  14.4 us
    ppermute x12, waiting for transfers between devices, permute(): return lax.ppermute(values, ('req', 'ctx'), pairs)  12.7 us
    unnamed x11, local copies, waits for them, and re-layouts  2.28 us
    pallas_call x2, Pallas kernels, shards(): pl.pallas_call(functools.partial(lookup_kernel, len(group)), in_specs=[VM...  1.47 us
    pallas_call x1, Pallas kernels, shards(): pl.pallas_call(functools.partial(finish_kernel, len(others)), grid=(1,),...  1.36 us
  transfers between devices with their start and end apart: 12, of which 6 were waited for; matrix products, arithmetic and copies ran while one was open for 0% of the time, Pallas kernels for 5%

profile of v5, /device:TPU:0, one launch (start us, length us, event | category | flops | bytes accessed | tf_op | source)
XLA Modules:
  0.0 58.0 jit_solution(13495930405230180230)
XLA Ops:
  0.0 0.7 %bitcast_or_fusion.packed_ref = s32[1,512]{1,0:T(1,128)S(1)} fusion(s32[1,512]{1,0:T(1,128)} %param.11, s32[1,512,1]{1,2,0:T(1,128)} %param.10), kind=kLoop, calls=%fused_computation.5 | loop fusion | flops 1024 | bytes 6144 | tf_op jit(solution)/shard_map/or | solution.py:285
  0.7 0.4 requests.1
  1.1 6.0 %collective-permute-start = (s32[1,128]{1,0:T(1,128)S(1)}, s32[1,128]{1,0:T(1,128)S(1)}, u32[]{:S(2)}, u32[]{:S(2)}) collective-permute-start(s32[1,128]{1,0:T(1,128)S(1)} %get-tuple-element.34), channel_id=1, source_target_pairs={{0,28},{1,25},{2,30},{3,27},{4,24},{5,29},{6,26},{7,31},{8,20},{9,... | collective-permute-start | bytes 1544 | tf_op jit(solution)/shard_map/ppermute | solution.py:277
  7.1 0.6 %collective-permute-start.4 = (s32[1,128]{1,0:T(1,128)S(1)}, s32[1,128]{1,0:T(1,128)S(1)}, u32[]{:S(2)}, u32[]{:S(2)}) collective-permute-start(s32[1,128]{1,0:T(1,128)S(1)} %get-tuple-element.39), channel_id=1, source_target_pairs={{0,12},{1,9},{2,14},{3,11},{4,8},{5,13},{6,10},{7,15},{8,4},{9,1},... | collective-permute-start | bytes 1544 | tf_op jit(solution)/shard_map/ppermute | solution.py:277
  7.8 0.6 %collective-permute-start.5 = (s32[1,128]{1,0:T(1,128)S(1)}, s32[1,128]{1,0:T(1,128)S(1)}, u32[]{:S(2)}, u32[]{:S(2)}) collective-permute-start(s32[1,128]{1,0:T(1,128)S(1)} %get-tuple-element.40), channel_id=1, source_target_pairs={{0,0},{1,5},{2,2},{3,7},{4,4},{5,1},{6,6},{7,3},{8,8},{9,13},{10,1... | collective-permute-start | bytes 1544 | tf_op jit(solution)/shard_map/ppermute | solution.py:277
  8.4 1.2 %copy-done.2 = bf16[2048,256]{1,0:T(8,128)(2,1)S(1)} copy-done((bf16[2048,256]{1,0:T(8,128)(2,1)S(1)}, bf16[2048,256]{1,0:T(8,128)(2,1)}, u32[]{:S(2)}) %copy-start.2) | copy-done | bytes 1048600
  9.7 1.8 %collective-permute-done.1.refs_1_ = s32[1,128]{1,0:T(1,128)S(1)} collective-permute-done((s32[1,128]{1,0:T(1,128)S(1)}, s32[1,128]{1,0:T(1,128)S(1)}, u32[]{:S(2)}, u32[]{:S(2)}) %collective-permute-start.1) | collective-permute-done | bytes 544 | tf_op jit(solution)/shard_map/ppermute | solution.py:277
  11.6 0.7 %lookup.2 = (bf16[128,256]{1,0:T(8,128)(2,1)S(1)}, bf16[128,256]{1,0:T(8,128)(2,1)S(1)}, bf16[8,128]{1,0:T(8,128)(2,1)S(1)}) custom-call(bf16[2048,256]{1,0:T(8,128)(2,1)S(1)} %get-tuple-element.32.table_ref, bf16[8,128]{1,0:T(8,128)(2,1)S(1)} %get-tuple-element.33.done_ref, s32[1,128]{1,0:T(1,128)S(1)} %collective-permute-done.refs_0_, ...), custom_call_target="tpu_custom_call" | custom-call | tf_op jit(solution)/shard_map/lookup/pallas_call | solution.py:306
  12.3 2.9 %collective-permute-start.2 = (bf16[128,256]{1,0:T(8,128)(2,1)S(1)}, bf16[128,256]{1,0:T(8,128)(2,1)S(1)}, u32[]{:S(2)}, u32[]{:S(2)}) collective-permute-start(bf16[128,256]{1,0:T(8,128)(2,1)S(1)} %get-tuple-element.36), channel_id=1, source_target_pairs={{0,28},{1,25},{2,30},{3,27},{4,24},{5,29},{6,26},{7,31},{8,20},{9,... | collective-permute-start | bytes 196616 | tf_op jit(solution)/shard_map/ppermute | solution.py:277
  15.2 0.7 %lookup.3 = (bf16[128,256]{1,0:T(8,128)(2,1)S(1)}, bf16[128,256]{1,0:T(8,128)(2,1)S(1)}, bf16[8,128]{1,0:T(8,128)(2,1)S(1)}) custom-call(bf16[2048,256]{1,0:T(8,128)(2,1)S(1)} %get-tuple-element.32.table_ref, bf16[8,128]{1,0:T(8,128)(2,1)S(1)} %get-tuple-element.38.done_ref, s32[1,128]{1,0:T(1,128)S(1)} %collective-permute-done.4.refs_0_, ...), custom_call_target="tpu_custom_call" | custom-call | tf_op jit(solution)/shard_map/lookup/pallas_call | solution.py:306
  15.9 2.5 %collective-permute-start.6 = (bf16[128,256]{1,0:T(8,128)(2,1)S(1)}, bf16[128,256]{1,0:T(8,128)(2,1)S(1)}, u32[]{:S(2)}, u32[]{:S(2)}) collective-permute-start(bf16[128,256]{1,0:T(8,128)(2,1)S(1)} %get-tuple-element.41), channel_id=1, source_target_pairs={{0,12},{1,9},{2,14},{3,11},{4,8},{5,13},{6,10},{7,15},{8,4},{9,1},... | collective-permute-start | bytes 196616 | tf_op jit(solution)/shard_map/ppermute | solution.py:277
  18.5 0.7 %collective-permute-start.7 = (bf16[128,256]{1,0:T(8,128)(2,1)S(1)}, bf16[128,256]{1,0:T(8,128)(2,1)S(1)}, u32[]{:S(2)}, u32[]{:S(2)}) collective-permute-start(bf16[128,256]{1,0:T(8,128)(2,1)S(1)} %get-tuple-element.42), channel_id=1, source_target_pairs={{0,0},{1,5},{2,2},{3,7},{4,4},{5,1},{6,6},{7,3},{8,8},{9,13},{10,1... | collective-permute-start | bytes 196616 | tf_op jit(solution)/shard_map/ppermute | solution.py:277
  19.1 1.0 %copy-done.3 = bf16[256,1024]{1,0:T(8,128)(2,1)S(1)} copy-done((bf16[256,1024]{1,0:T(8,128)(2,1)S(1)}, bf16[256,1024]{1,0:T(8,128)(2,1)}, u32[]{:S(2)}) %copy-start.3) | copy-done | bytes 524312
  20.2 0.7 %places.1 = (bf16[512,1024]{1,0:T(8,128)(2,1)S(1)}, bf16[256,1024]{1,0:T(8,128)(2,1)S(1)}) custom-call(s32[1,512]{1,0:T(1,128)S(1)} %bitcast_or_fusion.packed_ref, bf16[8,128]{1,0:T(8,128)(2,1)S(1)} %get-tuple-element.43.rows_ref, bf16[256,1024]{1,0:T(8,128)(2,1)S(1)} %copy-done.3), custom_call_target="tpu_custom_call" | custom-call | flops 268435456 | bytes 25165824 | tf_op jit(solution)/shard_map/places/pallas_call | solution.py:316
  21.2 1.0 %collective-permute-done.6 = bf16[128,256]{1,0:T(8,128)(2,1)S(1)} collective-permute-done((bf16[128,256]{1,0:T(8,128)(2,1)S(1)}, bf16[128,256]{1,0:T(8,128)(2,1)S(1)}, u32[]{:S(2)}, u32[]{:S(2)}) %collective-permute-start.6) | collective-permute-done | bytes 65568 | tf_op jit(solution)/shard_map/ppermute | solution.py:277
  22.3 0.3 collective-permute-start.8
  23.2 0.6 %collective-permute-done.8.refs_1_ = bf16[512,256]{1,0:T(8,128)(2,1)S(1)} collective-permute-done((bf16[512,256]{1,0:T(8,128)(2,1)S(1)}, bf16[512,256]{1,0:T(8,128)(2,1)S(1)}, u32[]{:S(2)}, u32[]{:S(2)}) %collective-permute-start.8) | collective-permute-done | bytes 262176 | tf_op jit(solution)/shard_map/ppermute | solution.py:277
  23.9 22.5 %attend.1 = (bf16[128,1024]{1,0:T(8,128)(2,1)S(1)}, bf16[128,1024]{1,0:T(8,128)(2,1)S(1)}, f32[8,256,128]{2,1,0:T(8,128)S(1)}, bf16[8,128,128]{2,1,0:T(8,128)(2,1)S(1)}, bf16[8,128,128]{2,1,0:T(8,128)(2,1)S(1)}) custom-call(s32[1]{0:T(128)S(6)} %copy.13.length_ref, bf16[512,1024]{1,0:T(8,128)(2,1)S(1)} %get-tuple-element.46.places_ref, ...), custom_call_target="tpu_custom_call" | custom-call | tf_op jit(solution)/shard_map/attend/pallas_call | solution.py:333
  46.4 0.3 collective-permute-start.9
  46.7 1.3 %collective-permute-done.9 = bf16[8,128,128]{2,1,0:T(8,128)(2,1)S(1)} collective-permute-done((bf16[8,128,128]{2,1,0:T(8,128)(2,1)S(1)}, bf16[8,128,128]{2,1,0:T(8,128)(2,1)S(1)}, u32[]{:S(2)}, u32[]{:S(2)}) %collective-permute-start.9) | collective-permute-done | bytes 262176 | tf_op jit(solution)/shard_map/ppermute | solution.py:277
  48.2 0.3 collective-permute-start.11
  48.5 0.5 gate.1.refs_3_
  49.0 7.6 %collective-permute-done.10.refs_1_ = bf16[8,128,128]{2,1,0:T(8,128)(2,1)S(1)} collective-permute-done((bf16[8,128,128]{2,1,0:T(8,128)(2,1)S(1)}, bf16[8,128,128]{2,1,0:T(8,128)(2,1)S(1)}, u32[]{:S(2)}, u32[]{:S(2)}) %collective-permute-start.10) | collective-permute-done | bytes 262176 | tf_op jit(solution)/shard_map/ppermute | solution.py:277
  56.6 1.4 %finish.1 = bf16[128,1024]{1,0:T(8,128)(2,1)} custom-call(f32[8,256,128]{2,1,0:T(8,128)S(1)} %get-tuple-element.52.refs_0_, bf16[8,128,128]{2,1,0:T(8,128)(2,1)S(1)} %collective-permute-done.10.refs_1_, bf16[8,128,128]{2,1,0:T(8,128)(2,1)S(1)} %collective-permute-done.11.refs_2_, bf16[128,1024]{1,0:T(8,128)(2,1)S(1)} %gate.1.refs_3_, ...), custom_call_target="tpu_custom_call" | custom-call | tf_op jit(solution)/shard_map/finish/pallas_call | solution.py:378
  (22 shorter events, 0.5 us)
Async XLA Ops:
  1.1 8.6 %collective-permute-start = (s32[1,128]{1,0:T(1,128)S(1)}, s32[1,128]{1,0:T(1,128)S(1)}, u32[]{:S(2)}, u32[]{:S(2)}) collective-permute-start(s32[1,128]{1,0:T(1,128)S(1)} %get-tuple-element.34), channel_id=1, source_target_pairs={{0,28},{1,25},{2,30},{3,27},{4,24},{5,29},{6,26},{7,31},{8,20},{9,... | collective-permute-start | bytes 1544 | tf_op jit(solution)/shard_map/ppermute | solution.py:277
  7.1 4.4 %collective-permute-start.1 = (s32[1,128]{1,0:T(1,128)S(1)}, s32[1,128]{1,0:T(1,128)S(1)}, u32[]{:S(2)}, u32[]{:S(2)}) collective-permute-start(s32[1,128]{1,0:T(1,128)S(1)} %get-tuple-element.35), channel_id=1, source_target_pairs={{0,16},{1,21},{2,18},{3,23},{4,20},{5,17},{6,22},{7,19},{8,24},{9,... | collective-permute-start | bytes 1544 | tf_op jit(solution)/shard_map/ppermute | solution.py:277
  7.1 8.1 %collective-permute-start.4 = (s32[1,128]{1,0:T(1,128)S(1)}, s32[1,128]{1,0:T(1,128)S(1)}, u32[]{:S(2)}, u32[]{:S(2)}) collective-permute-start(s32[1,128]{1,0:T(1,128)S(1)} %get-tuple-element.39), channel_id=1, source_target_pairs={{0,12},{1,9},{2,14},{3,11},{4,8},{5,13},{6,10},{7,15},{8,4},{9,1},... | collective-permute-start | bytes 1544 | tf_op jit(solution)/shard_map/ppermute | solution.py:277
  7.8 7.4 %collective-permute-start.5 = (s32[1,128]{1,0:T(1,128)S(1)}, s32[1,128]{1,0:T(1,128)S(1)}, u32[]{:S(2)}, u32[]{:S(2)}) collective-permute-start(s32[1,128]{1,0:T(1,128)S(1)} %get-tuple-element.40), channel_id=1, source_target_pairs={{0,0},{1,5},{2,2},{3,7},{4,4},{5,1},{6,6},{7,3},{8,8},{9,13},{10,1... | collective-permute-start | bytes 1544 | tf_op jit(solution)/shard_map/ppermute | solution.py:277
  8.4 1.2 %copy-start.2 = (bf16[2048,256]{1,0:T(8,128)(2,1)S(1)}, bf16[2048,256]{1,0:T(8,128)(2,1)}, u32[]{:S(2)}) copy-start(bf16[2048,256]{1,0:T(8,128)(2,1)} %table_ref.1) | copy-start | bytes 3145732
  12.3 8.6 %collective-permute-start.2 = (bf16[128,256]{1,0:T(8,128)(2,1)S(1)}, bf16[128,256]{1,0:T(8,128)(2,1)S(1)}, u32[]{:S(2)}, u32[]{:S(2)}) collective-permute-start(bf16[128,256]{1,0:T(8,128)(2,1)S(1)} %get-tuple-element.36), channel_id=1, source_target_pairs={{0,28},{1,25},{2,30},{3,27},{4,24},{5,29},{6,26},{7,31},{8,20},{9,... | collective-permute-start | bytes 196616 | tf_op jit(solution)/shard_map/ppermute | solution.py:277
  15.2 6.0 %collective-permute-start.3 = (bf16[128,256]{1,0:T(8,128)(2,1)S(1)}, bf16[128,256]{1,0:T(8,128)(2,1)S(1)}, u32[]{:S(2)}, u32[]{:S(2)}) collective-permute-start(bf16[128,256]{1,0:T(8,128)(2,1)S(1)} %get-tuple-element.37), channel_id=1, source_target_pairs={{0,16},{1,21},{2,18},{3,23},{4,20},{5,17},{6,22},{7,19},{8,24},{9,... | collective-permute-start | bytes 196616 | tf_op jit(solution)/shard_map/ppermute | solution.py:277
  15.9 6.3 %collective-permute-start.6 = (bf16[128,256]{1,0:T(8,128)(2,1)S(1)}, bf16[128,256]{1,0:T(8,128)(2,1)S(1)}, u32[]{:S(2)}, u32[]{:S(2)}) collective-permute-start(bf16[128,256]{1,0:T(8,128)(2,1)S(1)} %get-tuple-element.41), channel_id=1, source_target_pairs={{0,12},{1,9},{2,14},{3,11},{4,8},{5,13},{6,10},{7,15},{8,4},{9,1},... | collective-permute-start | bytes 196616 | tf_op jit(solution)/shard_map/ppermute | solution.py:277
  18.5 3.7 %collective-permute-start.7 = (bf16[128,256]{1,0:T(8,128)(2,1)S(1)}, bf16[128,256]{1,0:T(8,128)(2,1)S(1)}, u32[]{:S(2)}, u32[]{:S(2)}) collective-permute-start(bf16[128,256]{1,0:T(8,128)(2,1)S(1)} %get-tuple-element.42), channel_id=1, source_target_pairs={{0,0},{1,5},{2,2},{3,7},{4,4},{5,1},{6,6},{7,3},{8,8},{9,13},{10,1... | collective-permute-start | bytes 196616 | tf_op jit(solution)/shard_map/ppermute | solution.py:277
  19.1 1.0 %copy-start.3 = (bf16[256,1024]{1,0:T(8,128)(2,1)S(1)}, bf16[256,1024]{1,0:T(8,128)(2,1)}, u32[]{:S(2)}) copy-start(bf16[256,1024]{1,0:T(8,128)(2,1)} %w_in_ref.1) | copy-start | bytes 1572868
  22.3 1.6 %collective-permute-start.8 = (bf16[512,256]{1,0:T(8,128)(2,1)S(1)}, bf16[512,256]{1,0:T(8,128)(2,1)S(1)}, u32[]{:S(2)}, u32[]{:S(2)}) collective-permute-start(bf16[512,256]{1,0:T(8,128)(2,1)S(1)} %constant_dynamic-update-slice_fusion.refs_0_), channel_id=1, source_target_pairs={{0,1},{1,0},{2,3},{3,2},{4,5},{5,4},{6,7},{7,6},{8,9},{9,8},{10,11... | collective-permute-start | bytes 786440 | tf_op jit(solution)/shard_map/ppermute | solution.py:277
  23.9 24.6 %copy-start = (bf16[1024,2048]{1,0:T(8,128)(2,1)S(1)}, bf16[1024,2048]{1,0:T(8,128)(2,1)}, u32[]{:S(2)}) copy-start(bf16[1024,2048]{1,0:T(8,128)(2,1)} %w_uq_ref.1) | copy-start | bytes 12582916
  23.9 32.7 %copy-start.1 = (bf16[1024,1024]{1,0:T(8,128)(2,1)S(1)}, bf16[1024,1024]{1,0:T(8,128)(2,1)}, u32[]{:S(2)}) copy-start(bf16[1024,1024]{1,0:T(8,128)(2,1)} %refs_5_.1) | copy-start | bytes 6291460
  46.4 1.6 %collective-permute-start.9 = (bf16[8,128,128]{2,1,0:T(8,128)(2,1)S(1)}, bf16[8,128,128]{2,1,0:T(8,128)(2,1)S(1)}, u32[]{:S(2)}, u32[]{:S(2)}) collective-permute-start(bf16[8,128,128]{2,1,0:T(8,128)(2,1)S(1)} %get-tuple-element.54), channel_id=1, source_target_pairs={{0,1},{1,0},{2,3},{3,2},{4,5},{5,4},{6,7},{7,6},{8,9},{9,8},{10,11... | collective-permute-start | bytes 786440 | tf_op jit(solution)/shard_map/ppermute | solution.py:277
  48.1 8.5 %collective-permute-start.10 = (bf16[8,128,128]{2,1,0:T(8,128)(2,1)S(1)}, bf16[8,128,128]{2,1,0:T(8,128)(2,1)S(1)}, u32[]{:S(2)}, u32[]{:S(2)}) collective-permute-start(bf16[8,128,128]{2,1,0:T(8,128)(2,1)S(1)} %add_convert_fusion), channel_id=1, source_target_pairs={{0,2},{1,3},{2,0},{3,1},{4,6},{5,7},{6,4},{7,5},{8,10},{9,11},{10,... | collective-permute-start | bytes 786440 | tf_op jit(solution)/shard_map/ppermute | solution.py:277
  48.2 8.4 %collective-permute-start.11 = (bf16[8,128,128]{2,1,0:T(8,128)(2,1)S(1)}, bf16[8,128,128]{2,1,0:T(8,128)(2,1)S(1)}, u32[]{:S(2)}, u32[]{:S(2)}) collective-permute-start(bf16[8,128,128]{2,1,0:T(8,128)(2,1)S(1)} %get-tuple-element.56), channel_id=1, source_target_pairs={{0,1},{1,0},{2,3},{3,2},{4,5},{5,4},{6,7},{7,6},{8,9},{9,8},{10,11... | collective-permute-start | bytes 786440 | tf_op jit(solution)/shard_map/ppermute | solution.py:277

commit v6 on v5

--- a/solution.py
+++ b/solution.py
@@ -239,8 +239,9 @@
             )
 
 
-def gate_kernel(normed_ref, w_uq_ref, gate_ref):
+def gate_kernel(normed_ref, w_uq_ref, keep_ref, near_ref, gate_ref, base_ref):
     gate_ref[...] = silu(dot(normed_ref[...], w_uq_ref[...])).astype(BF16)
+    base_ref[...] = keep_ref[...] + near_ref[...].astype(F32)
 
 
 def finish_kernel(others, *refs):
@@ -352,19 +353,6 @@
         compiler_params=params(47),
         name="attend",
     )(hist_len, places, *buffers, w_in, w_uq, keys, values)
-    gate = pl.pallas_call(
-        gate_kernel,
-        grid=(1,),
-        in_specs=[
-            pl.BlockSpec((per, width), lambda i: (0, 0)),
-            pl.BlockSpec((width, width), lambda i: (0, 0)),
-        ],
-        out_specs=pl.BlockSpec((per, width), lambda i: (0, 0)),
-        out_shape=shape((per, width), BF16),
-        compiler_params=params(16),
-        cost_estimate=pl.CostEstimate(flops=1 << 28, bytes_accessed=3 << 20, transcendentals=0),
-        name="gate",
-    )(normed, w_uq)
     sibling = swap_peer(far, 1)
     sums = []
     for index in range(1, peers // 2):
@@ -373,8 +361,23 @@
         sums.append((kept + sibling[:, piece].astype(F32)).astype(BF16))
     near, *sums = lax.optimization_barrier((near, *sums))
     others = [swap_peer(one, 2 * index) for index, one in enumerate(sums, 1)]
-    others.append(swap_peer(near, 1))
+    near = swap_peer(near, 1)
     block = pl.BlockSpec((HEADS, per, head_dim), lambda i: (0, 0, 0))
+    gate, base = pl.pallas_call(
+        gate_kernel,
+        grid=(1,),
+        in_specs=[
+            pl.BlockSpec((per, width), lambda i: (0, 0)),
+            pl.BlockSpec((width, width), lambda i: (0, 0)),
+            block,
+            block,
+        ],
+        out_specs=[pl.BlockSpec((per, width), lambda i: (0, 0)), block],
+        out_shape=[shape((per, width), BF16), shape((HEADS, per, head_dim), F32)],
+        compiler_params=params(16),
+        cost_estimate=pl.CostEstimate(flops=1 << 28, bytes_accessed=3 << 20, transcendentals=0),
+        name="gate",
+    )(normed, w_uq, keep, near)
     ranked = pl.pallas_call(
         functools.partial(finish_kernel, len(others)),
         grid=(1,),
@@ -385,7 +388,7 @@
         out_shape=shape((per, width), BF16),
         compiler_params=params(24),
         name="finish",
-    )(keep, *others, gate, features, w_out)
+    )(base, *others, gate, features, w_out)
     return ranked[None]
 
 

time: 58.7 us -> 58.9 us (level)
  transfers between devices with their start and end apart: 12 -> 12, of which waited for: 6 -> 7; matrix products, arithmetic and copies ran while one was open for 0% -> 0% of each run, Pallas kernels for 5% -> 5%
where the time goes in v6:
time: 58.9 us; the launch traced here: 58.2 us
  Pallas kernels  27 us (46%)
  starting transfers between devices  14.3 us (24%)
  waiting for transfers between devices  13 us (22%)
  local copies, waits for them, and re-layouts  2.29 us (4%)
  between operations  0.79 us (1%)
  other arithmetic  0.77 us (1%)
    pallas_call x1, Pallas kernels, shards(): pl.pallas_call(functools.partial(attend_kernel, per, len(buffers)), in_sp...  22.5 us
    ppermute x12, starting transfers between devices, permute(): return lax.ppermute(values, ('req', 'ctx'), pairs)  14.3 us
    ppermute x12, waiting for transfers between devices, permute(): return lax.ppermute(values, ('req', 'ctx'), pairs)  13 us
    unnamed x11, local copies, waits for them, and re-layouts  2.28 us
    pallas_call x2, Pallas kernels, shards(): pl.pallas_call(functools.partial(lookup_kernel, len(group)), in_specs=[VM...  1.47 us
    pallas_call x1, Pallas kernels, shards(): pl.pallas_call(functools.partial(finish_kernel, len(others)), grid=(1,),...  1.32 us
  transfers between devices with their start and end apart: 12, of which 7 were waited for; matrix products, arithmetic and copies ran while one was open for 0% of the time, Pallas kernels for 5%

profile of v6, /device:TPU:0, one launch (start us, length us, event | category | flops | bytes accessed | tf_op | source)
XLA Modules:
  0.0 58.2 jit_solution(16178798438800159689)
XLA Ops:
  0.0 0.7 %bitcast_or_fusion.packed_ref = s32[1,512]{1,0:T(1,128)S(1)} fusion(s32[1,512]{1,0:T(1,128)} %param.11, s32[1,512,1]{1,2,0:T(1,128)} %param.10), kind=kLoop, calls=%fused_computation.5 | loop fusion | flops 1024 | bytes 6144 | tf_op jit(solution)/shard_map/or | solution.py:286
  0.7 0.4 requests.1
  1.1 6.0 %collective-permute-start = (s32[1,128]{1,0:T(1,128)S(1)}, s32[1,128]{1,0:T(1,128)S(1)}, u32[]{:S(2)}, u32[]{:S(2)}) collective-permute-start(s32[1,128]{1,0:T(1,128)S(1)} %get-tuple-element.36), channel_id=1, source_target_pairs={{0,28},{1,25},{2,30},{3,27},{4,24},{5,29},{6,26},{7,31},{8,20},{9,... | collective-permute-start | bytes 1544 | tf_op jit(solution)/shard_map/ppermute | solution.py:278
  7.1 0.6 %collective-permute-start.4 = (s32[1,128]{1,0:T(1,128)S(1)}, s32[1,128]{1,0:T(1,128)S(1)}, u32[]{:S(2)}, u32[]{:S(2)}) collective-permute-start(s32[1,128]{1,0:T(1,128)S(1)} %get-tuple-element.41), channel_id=1, source_target_pairs={{0,12},{1,9},{2,14},{3,11},{4,8},{5,13},{6,10},{7,15},{8,4},{9,1},... | collective-permute-start | bytes 1544 | tf_op jit(solution)/shard_map/ppermute | solution.py:278
  7.8 0.6 %collective-permute-start.5 = (s32[1,128]{1,0:T(1,128)S(1)}, s32[1,128]{1,0:T(1,128)S(1)}, u32[]{:S(2)}, u32[]{:S(2)}) collective-permute-start(s32[1,128]{1,0:T(1,128)S(1)} %get-tuple-element.42), channel_id=1, source_target_pairs={{0,0},{1,5},{2,2},{3,7},{4,4},{5,1},{6,6},{7,3},{8,8},{9,13},{10,1... | collective-permute-start | bytes 1544 | tf_op jit(solution)/shard_map/ppermute | solution.py:278
  8.4 1.2 %copy-done.2 = bf16[2048,256]{1,0:T(8,128)(2,1)S(1)} copy-done((bf16[2048,256]{1,0:T(8,128)(2,1)S(1)}, bf16[2048,256]{1,0:T(8,128)(2,1)}, u32[]{:S(2)}) %copy-start.2) | copy-done | bytes 1048600
  9.7 1.8 %collective-permute-done.1.refs_1_ = s32[1,128]{1,0:T(1,128)S(1)} collective-permute-done((s32[1,128]{1,0:T(1,128)S(1)}, s32[1,128]{1,0:T(1,128)S(1)}, u32[]{:S(2)}, u32[]{:S(2)}) %collective-permute-start.1) | collective-permute-done | bytes 544 | tf_op jit(solution)/shard_map/ppermute | solution.py:278
  11.6 0.7 %lookup.2 = (bf16[128,256]{1,0:T(8,128)(2,1)S(1)}, bf16[128,256]{1,0:T(8,128)(2,1)S(1)}, bf16[8,128]{1,0:T(8,128)(2,1)S(1)}) custom-call(bf16[2048,256]{1,0:T(8,128)(2,1)S(1)} %get-tuple-element.34.table_ref, bf16[8,128]{1,0:T(8,128)(2,1)S(1)} %get-tuple-element.35.done_ref, s32[1,128]{1,0:T(1,128)S(1)} %collective-permute-done.refs_0_, ...), custom_call_target="tpu_custom_call" | custom-call | tf_op jit(solution)/shard_map/lookup/pallas_call | solution.py:307
  12.3 2.9 %collective-permute-start.2 = (bf16[128,256]{1,0:T(8,128)(2,1)S(1)}, bf16[128,256]{1,0:T(8,128)(2,1)S(1)}, u32[]{:S(2)}, u32[]{:S(2)}) collective-permute-start(bf16[128,256]{1,0:T(8,128)(2,1)S(1)} %get-tuple-element.38), channel_id=1, source_target_pairs={{0,28},{1,25},{2,30},{3,27},{4,24},{5,29},{6,26},{7,31},{8,20},{9,... | collective-permute-start | bytes 196616 | tf_op jit(solution)/shard_map/ppermute | solution.py:278
  15.2 0.7 %lookup.3 = (bf16[128,256]{1,0:T(8,128)(2,1)S(1)}, bf16[128,256]{1,0:T(8,128)(2,1)S(1)}, bf16[8,128]{1,0:T(8,128)(2,1)S(1)}) custom-call(bf16[2048,256]{1,0:T(8,128)(2,1)S(1)} %get-tuple-element.34.table_ref, bf16[8,128]{1,0:T(8,128)(2,1)S(1)} %get-tuple-element.40.done_ref, s32[1,128]{1,0:T(1,128)S(1)} %collective-permute-done.4.refs_0_, ...), custom_call_target="tpu_custom_call" | custom-call | tf_op jit(solution)/shard_map/lookup/pallas_call | solution.py:307
  15.9 2.5 %collective-permute-start.6 = (bf16[128,256]{1,0:T(8,128)(2,1)S(1)}, bf16[128,256]{1,0:T(8,128)(2,1)S(1)}, u32[]{:S(2)}, u32[]{:S(2)}) collective-permute-start(bf16[128,256]{1,0:T(8,128)(2,1)S(1)} %get-tuple-element.43), channel_id=1, source_target_pairs={{0,12},{1,9},{2,14},{3,11},{4,8},{5,13},{6,10},{7,15},{8,4},{9,1},... | collective-permute-start | bytes 196616 | tf_op jit(solution)/shard_map/ppermute | solution.py:278
  18.5 0.7 %collective-permute-start.7 = (bf16[128,256]{1,0:T(8,128)(2,1)S(1)}, bf16[128,256]{1,0:T(8,128)(2,1)S(1)}, u32[]{:S(2)}, u32[]{:S(2)}) collective-permute-start(bf16[128,256]{1,0:T(8,128)(2,1)S(1)} %get-tuple-element.44), channel_id=1, source_target_pairs={{0,0},{1,5},{2,2},{3,7},{4,4},{5,1},{6,6},{7,3},{8,8},{9,13},{10,1... | collective-permute-start | bytes 196616 | tf_op jit(solution)/shard_map/ppermute | solution.py:278
  19.1 1.0 %copy-done.3 = bf16[256,1024]{1,0:T(8,128)(2,1)S(1)} copy-done((bf16[256,1024]{1,0:T(8,128)(2,1)S(1)}, bf16[256,1024]{1,0:T(8,128)(2,1)}, u32[]{:S(2)}) %copy-start.3) | copy-done | bytes 524312
  20.2 0.7 %places.1 = (bf16[512,1024]{1,0:T(8,128)(2,1)S(1)}, bf16[256,1024]{1,0:T(8,128)(2,1)S(1)}) custom-call(s32[1,512]{1,0:T(1,128)S(1)} %bitcast_or_fusion.packed_ref, bf16[8,128]{1,0:T(8,128)(2,1)S(1)} %get-tuple-element.45.rows_ref, bf16[256,1024]{1,0:T(8,128)(2,1)S(1)} %copy-done.3), custom_call_target="tpu_custom_call" | custom-call | flops 268435456 | bytes 25165824 | tf_op jit(solution)/shard_map/places/pallas_call | solution.py:317
  21.2 1.0 %collective-permute-done.6 = bf16[128,256]{1,0:T(8,128)(2,1)S(1)} collective-permute-done((bf16[128,256]{1,0:T(8,128)(2,1)S(1)}, bf16[128,256]{1,0:T(8,128)(2,1)S(1)}, u32[]{:S(2)}, u32[]{:S(2)}) %collective-permute-start.6) | collective-permute-done | bytes 65568 | tf_op jit(solution)/shard_map/ppermute | solution.py:278
  22.3 0.3 collective-permute-start.8
  23.2 0.6 %collective-permute-done.8.refs_1_ = bf16[512,256]{1,0:T(8,128)(2,1)S(1)} collective-permute-done((bf16[512,256]{1,0:T(8,128)(2,1)S(1)}, bf16[512,256]{1,0:T(8,128)(2,1)S(1)}, u32[]{:S(2)}, u32[]{:S(2)}) %collective-permute-start.8) | collective-permute-done | bytes 262176 | tf_op jit(solution)/shard_map/ppermute | solution.py:278
  23.9 22.5 %attend.1 = (bf16[128,1024]{1,0:T(8,128)(2,1)S(1)}, bf16[128,1024]{1,0:T(8,128)(2,1)S(1)}, f32[8,256,128]{2,1,0:T(8,128)S(1)}, bf16[8,128,128]{2,1,0:T(8,128)(2,1)S(1)}, bf16[8,128,128]{2,1,0:T(8,128)(2,1)S(1)}) custom-call(s32[1]{0:T(128)S(6)} %copy.13.length_ref, bf16[512,1024]{1,0:T(8,128)(2,1)S(1)} %get-tuple-element.48.places_ref, ...), custom_call_target="tpu_custom_call" | custom-call | tf_op jit(solution)/shard_map/attend/pallas_call | solution.py:334
  46.4 0.3 collective-permute-start.9
  46.7 1.3 %collective-permute-done.9 = bf16[8,128,128]{2,1,0:T(8,128)(2,1)S(1)} collective-permute-done((bf16[8,128,128]{2,1,0:T(8,128)(2,1)S(1)}, bf16[8,128,128]{2,1,0:T(8,128)(2,1)S(1)}, u32[]{:S(2)}, u32[]{:S(2)}) %collective-permute-start.9) | collective-permute-done | bytes 262176 | tf_op jit(solution)/shard_map/ppermute | solution.py:278
  48.4 1.3 %collective-permute-done.10.near_ref = bf16[8,128,128]{2,1,0:T(8,128)(2,1)S(1)} collective-permute-done((bf16[8,128,128]{2,1,0:T(8,128)(2,1)S(1)}, bf16[8,128,128]{2,1,0:T(8,128)(2,1)S(1)}, u32[]{:S(2)}, u32[]{:S(2)}) %collective-permute-start.10) | collective-permute-done | bytes 262176 | tf_op jit(solution)/shard_map/ppermute | solution.py:278
  49.7 0.5 gate.1
  50.2 6.7 %collective-permute-done.11.refs_1_ = bf16[8,128,128]{2,1,0:T(8,128)(2,1)S(1)} collective-permute-done((bf16[8,128,128]{2,1,0:T(8,128)(2,1)S(1)}, bf16[8,128,128]{2,1,0:T(8,128)(2,1)S(1)}, u32[]{:S(2)}, u32[]{:S(2)}) %collective-permute-start.11) | collective-permute-done | bytes 262176 | tf_op jit(solution)/shard_map/ppermute | solution.py:278
  56.9 1.3 %finish.1 = bf16[128,1024]{1,0:T(8,128)(2,1)} custom-call(f32[8,128,128]{2,1,0:T(8,128)S(1)} %get-tuple-element.59.refs_0_, bf16[8,128,128]{2,1,0:T(8,128)(2,1)S(1)} %collective-permute-done.11.refs_1_, bf16[128,1024]{1,0:T(8,128)(2,1)S(1)} %get-tuple-element.61.refs_2_, bf16[128,1024]{1,0:T(8,128)(2,1)S(1)} %get-tuple-element.62.refs_3_, ...), custom_call_target="tpu_custom_call" | custom-call | tf_op jit(solution)/shard_map/finish/pallas_call | solution.py:381
  (22 shorter events, 0.8 us)
Async XLA Ops:
  1.1 8.6 %collective-permute-start = (s32[1,128]{1,0:T(1,128)S(1)}, s32[1,128]{1,0:T(1,128)S(1)}, u32[]{:S(2)}, u32[]{:S(2)}) collective-permute-start(s32[1,128]{1,0:T(1,128)S(1)} %get-tuple-element.36), channel_id=1, source_target_pairs={{0,28},{1,25},{2,30},{3,27},{4,24},{5,29},{6,26},{7,31},{8,20},{9,... | collective-permute-start | bytes 1544 | tf_op jit(solution)/shard_map/ppermute | solution.py:278
  7.1 4.4 %collective-permute-start.1 = (s32[1,128]{1,0:T(1,128)S(1)}, s32[1,128]{1,0:T(1,128)S(1)}, u32[]{:S(2)}, u32[]{:S(2)}) collective-permute-start(s32[1,128]{1,0:T(1,128)S(1)} %get-tuple-element.37), channel_id=1, source_target_pairs={{0,16},{1,21},{2,18},{3,23},{4,20},{5,17},{6,22},{7,19},{8,24},{9,... | collective-permute-start | bytes 1544 | tf_op jit(solution)/shard_map/ppermute | solution.py:278
  7.1 8.1 %collective-permute-start.4 = (s32[1,128]{1,0:T(1,128)S(1)}, s32[1,128]{1,0:T(1,128)S(1)}, u32[]{:S(2)}, u32[]{:S(2)}) collective-permute-start(s32[1,128]{1,0:T(1,128)S(1)} %get-tuple-element.41), channel_id=1, source_target_pairs={{0,12},{1,9},{2,14},{3,11},{4,8},{5,13},{6,10},{7,15},{8,4},{9,1},... | collective-permute-start | bytes 1544 | tf_op jit(solution)/shard_map/ppermute | solution.py:278
  7.8 7.4 %collective-permute-start.5 = (s32[1,128]{1,0:T(1,128)S(1)}, s32[1,128]{1,0:T(1,128)S(1)}, u32[]{:S(2)}, u32[]{:S(2)}) collective-permute-start(s32[1,128]{1,0:T(1,128)S(1)} %get-tuple-element.42), channel_id=1, source_target_pairs={{0,0},{1,5},{2,2},{3,7},{4,4},{5,1},{6,6},{7,3},{8,8},{9,13},{10,1... | collective-permute-start | bytes 1544 | tf_op jit(solution)/shard_map/ppermute | solution.py:278
  8.4 1.2 %copy-start.2 = (bf16[2048,256]{1,0:T(8,128)(2,1)S(1)}, bf16[2048,256]{1,0:T(8,128)(2,1)}, u32[]{:S(2)}) copy-start(bf16[2048,256]{1,0:T(8,128)(2,1)} %table_ref.1) | copy-start | bytes 3145732
  12.3 8.6 %collective-permute-start.2 = (bf16[128,256]{1,0:T(8,128)(2,1)S(1)}, bf16[128,256]{1,0:T(8,128)(2,1)S(1)}, u32[]{:S(2)}, u32[]{:S(2)}) collective-permute-start(bf16[128,256]{1,0:T(8,128)(2,1)S(1)} %get-tuple-element.38), channel_id=1, source_target_pairs={{0,28},{1,25},{2,30},{3,27},{4,24},{5,29},{6,26},{7,31},{8,20},{9,... | collective-permute-start | bytes 196616 | tf_op jit(solution)/shard_map/ppermute | solution.py:278
  15.2 6.0 %collective-permute-start.3 = (bf16[128,256]{1,0:T(8,128)(2,1)S(1)}, bf16[128,256]{1,0:T(8,128)(2,1)S(1)}, u32[]{:S(2)}, u32[]{:S(2)}) collective-permute-start(bf16[128,256]{1,0:T(8,128)(2,1)S(1)} %get-tuple-element.39), channel_id=1, source_target_pairs={{0,16},{1,21},{2,18},{3,23},{4,20},{5,17},{6,22},{7,19},{8,24},{9,... | collective-permute-start | bytes 196616 | tf_op jit(solution)/shard_map/ppermute | solution.py:278
  15.9 6.3 %collective-permute-start.6 = (bf16[128,256]{1,0:T(8,128)(2,1)S(1)}, bf16[128,256]{1,0:T(8,128)(2,1)S(1)}, u32[]{:S(2)}, u32[]{:S(2)}) collective-permute-start(bf16[128,256]{1,0:T(8,128)(2,1)S(1)} %get-tuple-element.43), channel_id=1, source_target_pairs={{0,12},{1,9},{2,14},{3,11},{4,8},{5,13},{6,10},{7,15},{8,4},{9,1},... | collective-permute-start | bytes 196616 | tf_op jit(solution)/shard_map/ppermute | solution.py:278
  18.5 3.7 %collective-permute-start.7 = (bf16[128,256]{1,0:T(8,128)(2,1)S(1)}, bf16[128,256]{1,0:T(8,128)(2,1)S(1)}, u32[]{:S(2)}, u32[]{:S(2)}) collective-permute-start(bf16[128,256]{1,0:T(8,128)(2,1)S(1)} %get-tuple-element.44), channel_id=1, source_target_pairs={{0,0},{1,5},{2,2},{3,7},{4,4},{5,1},{6,6},{7,3},{8,8},{9,13},{10,1... | collective-permute-start | bytes 196616 | tf_op jit(solution)/shard_map/ppermute | solution.py:278
  19.1 1.0 %copy-start.3 = (bf16[256,1024]{1,0:T(8,128)(2,1)S(1)}, bf16[256,1024]{1,0:T(8,128)(2,1)}, u32[]{:S(2)}) copy-start(bf16[256,1024]{1,0:T(8,128)(2,1)} %w_in_ref.1) | copy-start | bytes 1572868
  22.3 1.6 %collective-permute-start.8 = (bf16[512,256]{1,0:T(8,128)(2,1)S(1)}, bf16[512,256]{1,0:T(8,128)(2,1)S(1)}, u32[]{:S(2)}, u32[]{:S(2)}) collective-permute-start(bf16[512,256]{1,0:T(8,128)(2,1)S(1)} %constant_dynamic-update-slice_fusion.refs_0_), channel_id=1, source_target_pairs={{0,1},{1,0},{2,3},{3,2},{4,5},{5,4},{6,7},{7,6},{8,9},{9,8},{10,11... | collective-permute-start | bytes 786440 | tf_op jit(solution)/shard_map/ppermute | solution.py:278
  23.9 25.8 %copy-start = (bf16[1024,2048]{1,0:T(8,128)(2,1)S(1)}, bf16[1024,2048]{1,0:T(8,128)(2,1)}, u32[]{:S(2)}) copy-start(bf16[1024,2048]{1,0:T(8,128)(2,1)} %w_uq_ref.1) | copy-start | bytes 12582916
  23.9 33.0 %copy-start.1 = (bf16[1024,1024]{1,0:T(8,128)(2,1)S(1)}, bf16[1024,1024]{1,0:T(8,128)(2,1)}, u32[]{:S(2)}) copy-start(bf16[1024,1024]{1,0:T(8,128)(2,1)} %refs_4_.1) | copy-start | bytes 6291460
  46.4 1.6 %collective-permute-start.9 = (bf16[8,128,128]{2,1,0:T(8,128)(2,1)S(1)}, bf16[8,128,128]{2,1,0:T(8,128)(2,1)S(1)}, u32[]{:S(2)}, u32[]{:S(2)}) collective-permute-start(bf16[8,128,128]{2,1,0:T(8,128)(2,1)S(1)} %get-tuple-element.57), channel_id=1, source_target_pairs={{0,1},{1,0},{2,3},{3,2},{4,5},{5,4},{6,7},{7,6},{8,9},{9,8},{10,11... | collective-permute-start | bytes 786440 | tf_op jit(solution)/shard_map/ppermute | solution.py:278
  48.1 1.6 %collective-permute-start.10 = (bf16[8,128,128]{2,1,0:T(8,128)(2,1)S(1)}, bf16[8,128,128]{2,1,0:T(8,128)(2,1)S(1)}, u32[]{:S(2)}, u32[]{:S(2)}) collective-permute-start(bf16[8,128,128]{2,1,0:T(8,128)(2,1)S(1)} %get-tuple-element.58), channel_id=1, source_target_pairs={{0,1},{1,0},{2,3},{3,2},{4,5},{5,4},{6,7},{7,6},{8,9},{9,8},{10,11... | collective-permute-start | bytes 786440 | tf_op jit(solution)/shard_map/ppermute | solution.py:278
  48.4 8.5 %collective-permute-start.11 = (bf16[8,128,128]{2,1,0:T(8,128)(2,1)S(1)}, bf16[8,128,128]{2,1,0:T(8,128)(2,1)S(1)}, u32[]{:S(2)}, u32[]{:S(2)}) collective-permute-start(bf16[8,128,128]{2,1,0:T(8,128)(2,1)S(1)} %add_convert_fusion), channel_id=1, source_target_pairs={{0,2},{1,3},{2,0},{3,1},{4,6},{5,7},{6,4},{7,5},{8,10},{9,11},{10,... | collective-permute-start | bytes 786440 | tf_op jit(solution)/shard_map/ppermute | solution.py:278
